TPU v7x, 32 devices: a whole 2x2x4 slice. The times are simulated.
32 devices in a mesh: clip: 4 (over y, x), frame: 4 (over z), tile: 2 (over core).
Axes of the slice: x: 2, y: 2, z: 4, core: 2. Of those that a mesh axis runs over, the one named last changes fastest.
Arguments:
- clip_feats: bfloat16 [128, 8, 16, 256], P(('clip', 'frame'), 'tile'), parts along dimension 0, may hold values from -6 to 6
- out_grad: bfloat16 [128, 8, 16, 256], P(('clip', 'frame'), 'tile'), parts along dimension 0, may hold values from -6 to 6
- spatial_weight: bfloat16 [2304, 256], replicated, may hold values from -0.125 to 0.125
- temporal_weight: bfloat16 [2304, 256], replicated, may hold values from -0.125 to 0.125
Outputs:
- block_out: bfloat16 [128, 8, 16, 256], P(('clip', 'frame'), 'tile'), parts along dimension 0
- input_grad: bfloat16 [128, 8, 16, 256], P(('clip', 'frame'), 'tile'), parts along dimension 0
- weight_grad: float32 [9216, 256], P(('clip', 'frame', 'tile')), parts along dimension 0
There are 4 independent parts, one for each index of `clip`. A program takes and returns all parts, laid end to end along the dimension named above; an argument that names none is the same for every part. Nothing has to cross between parts.
All inputs are finite; a program needn't handle non-finite values.
Results may differ from a plain program's by a relative error of at most 0.009.
Values may be sent and summed in bfloat16 or wider, within the bound.
No kernel may reach another device: no remote copies, remote signals or barrier semaphores. Data moves between devices by JAX's collectives and lax.ppermute only.
A program may use at most 64 MiB of HBM per device.

v0:
```python
import functools
import math

import jax
import jax.numpy as jnp
from jax import lax
from jax.experimental import pallas as pl
from jax.experimental.pallas import tpu as pltpu
from jax.sharding import PartitionSpec as P

TAP_DILATION = 2
VMEM_LIMIT = 32 * 1024 * 1024


def padded_2(block, sides, width):
    for axis, dim in sides:
        count = lax.axis_size(axis)
        forward = [(i, i + 1) for i in range(count - 1)]
        backward = [(target, source) for source, target in forward]
        low = lax.ppermute(
            lax.slice_in_dim(block, block.shape[dim] - width, None, axis=dim), axis, forward
        )
        high = lax.ppermute(lax.slice_in_dim(block, 0, width, axis=dim), axis, backward)
        block = jnp.concatenate([low, block, high], axis=dim)
    return block


def tile_columns(extended, tile_rows, width_cells, backward_pass):
    padded = jnp.pad(extended, ((0, 0), (0, 0), (1, 1), (0, 0)))
    pieces = []
    for row_shift in range(3):
        for col_shift in range(3):
            row_start = 2 - row_shift if backward_pass else row_shift
            col_start = 2 - col_shift if backward_pass else col_shift
            pieces.append(
                padded[:, row_start : row_start + tile_rows, col_start : col_start + width_cells, :]
            )
    channels = extended.shape[3]
    return jnp.concatenate(pieces, axis=-1).reshape(-1, 9 * channels)


def temporal_taps(padded_seq, weight, frame_count, backward_pass):
    pieces = []
    for temporal_tap_index in range(9):
        first_frame_index = (
            (8 - temporal_tap_index) * TAP_DILATION
            if backward_pass
            else temporal_tap_index * TAP_DILATION
        )
        pieces.append(padded_seq[first_frame_index : first_frame_index + frame_count])
    channels = padded_seq.shape[2]
    columns = jnp.concatenate(pieces, axis=-1).reshape(-1, 9 * channels)
    return jnp.dot(columns, weight, preferred_element_type=jnp.float32)


def per_device_any(clip_feats, out_grad, spatial_weight, temporal_weight):
    slab_frames, tile_rows, width_cells, channels = clip_feats.shape
    row_count = slab_frames * tile_rows * width_cells
    frame_devs = lax.axis_size("frame")
    tile_devs = lax.axis_size("tile")
    grad_scale = jnp.float32(
        1.0 / math.sqrt(slab_frames * frame_devs * tile_rows * tile_devs * width_cells)
    )
    spatial_back = (
        spatial_weight.reshape(9, channels, channels)
        .transpose(0, 2, 1)
        .reshape(9 * channels, channels)
    )
    temporal_back = (
        temporal_weight.reshape(9, channels, channels)
        .transpose(0, 2, 1)
        .reshape(9 * channels, channels)
    )
    feat_ext = padded_2(clip_feats, (("tile", 1),), 1)
    feat_columns = tile_columns(feat_ext, tile_rows, width_cells, False)
    pre = jnp.dot(feat_columns, spatial_weight, preferred_element_type=jnp.float32)
    act = jax.nn.silu(pre).astype(jnp.bfloat16)
    temporal_reach = 4 * TAP_DILATION
    per_group = tile_rows * width_cells // frame_devs
    grouped = (slab_frames, frame_devs, per_group, channels)
    act_part = lax.all_to_all(
        act.reshape(grouped), "frame", split_axis=1, concat_axis=0, tiled=True
    )
    grad_part = lax.all_to_all(out_grad, "frame", split_axis=1, concat_axis=0, tiled=True)
    feat_part = lax.all_to_all(clip_feats, "frame", split_axis=1, concat_axis=0, tiled=True)
    frame_count = act_part.shape[0]
    item_count = act_part.shape[2]
    act_pad = jnp.pad(
        act_part.reshape(frame_count, item_count, channels),
        ((temporal_reach, temporal_reach), (0, 0), (0, 0)),
    )
    grad_pad = jnp.pad(
        grad_part.reshape(frame_count, item_count, channels),
        ((temporal_reach, temporal_reach), (0, 0), (0, 0)),
    )
    mixed = temporal_taps(act_pad, temporal_weight, frame_count, False)
    out_part = (feat_part.reshape(-1, channels).astype(jnp.float32) + mixed).astype(jnp.bfloat16)
    back_part = temporal_taps(grad_pad, temporal_back, frame_count, True).astype(jnp.bfloat16)
    out_part = out_part.reshape(frame_count, 1, item_count, channels)
    back_part = back_part.reshape(frame_count, 1, item_count, channels)
    out_slab = lax.all_to_all(out_part, "frame", split_axis=0, concat_axis=1, tiled=True)
    grad_slab = lax.all_to_all(back_part, "frame", split_axis=0, concat_axis=1, tiled=True)
    act_grad = grad_slab.reshape(row_count, channels)
    sig = jax.nn.sigmoid(pre)
    pre_grad = (act_grad.astype(jnp.float32) * (sig * (1.0 + pre * (1.0 - sig)))).astype(
        jnp.bfloat16
    )
    full_term = lax.dot_general(
        feat_columns, pre_grad, (((0,), (0,)), ((), ())), preferred_element_type=jnp.float32
    )
    summed = lax.psum_scatter(full_term, ("frame", "tile"), scatter_dimension=0, tiled=True)
    weight_grad = summed * grad_scale
    grad_ext = padded_2(
        pre_grad.reshape(slab_frames, tile_rows, width_cells, channels), (("tile", 1),), 1
    )
    grad_columns = tile_columns(grad_ext, tile_rows, width_cells, True)
    local_back = jnp.dot(grad_columns, spatial_back, preferred_element_type=jnp.float32)
    input_grad = (out_grad.reshape(row_count, channels).astype(jnp.float32) + local_back).astype(
        jnp.bfloat16
    )
    input_grad = input_grad.reshape(slab_frames, tile_rows, width_cells, channels)
    return (out_slab, input_grad, weight_grad)


def kernel_call(body, outs, scratch, flops, *args, anywhere=0):
    moved = sum(a.size * a.dtype.itemsize for a in args)
    moved += sum(math.prod(shape) * jnp.dtype(kind).itemsize for shape, kind in outs)
    spaces = [pltpu.VMEM] * (len(args) - anywhere) + [pl.ANY] * anywhere
    return pl.pallas_call(
        body,
        out_shape=tuple(jax.ShapeDtypeStruct(shape, kind) for shape, kind in outs),
        in_specs=[pl.BlockSpec(memory_space=space) for space in spaces],
        out_specs=tuple(pl.BlockSpec(memory_space=pltpu.VMEM) for _ in outs),
        scratch_shapes=[pltpu.VMEM(shape, kind) for shape, kind in scratch],
        compiler_params=pltpu.CompilerParams(vmem_limit_bytes=VMEM_LIMIT),
        cost_estimate=pl.CostEstimate(flops=flops, bytes_accessed=moved, transcendentals=0),
    )(*args)


def shifted(values, width, step):
    rows = values.shape[0]
    at = lax.broadcasted_iota(jnp.int32, values.shape, 0) % width
    moved = pltpu.roll(values, step % rows, 0)
    inside = at >= step if step > 0 else at < width + step
    return jnp.where(inside, moved, 0.0)


def column_shifts(values, width):
    wide = values.astype(jnp.float32)
    return (
        shifted(wide, width, 1).astype(values.dtype),
        values,
        shifted(wide, width, -1).astype(values.dtype),
    )


def with_edges(own, other, ext):
    rows = own.shape[1]
    tile = lax.axis_index("tile")
    ext[:, 1 : rows + 1] = own[...]
    above, below = other[:, rows - 1], other[:, 0]
    ext[:, 0] = jnp.where(tile == 1, above, jnp.zeros_like(above))
    ext[:, rows + 1] = jnp.where(tile == 0, below, jnp.zeros_like(below))


def whole_image(own, other, image):
    rows = own.shape[1]
    tile = lax.axis_index("tile")
    image[:, 0] = jnp.zeros_like(image[:, 0])
    image[:, 2 * rows + 1] = jnp.zeros_like(image[:, 2 * rows + 1])
    image[:, pl.ds(1 + tile * rows, rows)] = own[...]
    image[:, pl.ds(1 + (1 - tile) * rows, rows)] = other[...]


def first_kernel(out_ref):
    out_ref[...] = jnp.zeros_like(out_ref)


def spatial_kernel(own, weight, other, _, pre_ref, act_ref, image, pre_all):
    frames, rows, width, channels = own.shape
    whole_image(own, other, image)
    shifts = column_shifts(image[...].reshape(-1, channels), width)
    shifts = [piece.reshape(image.shape) for piece in shifts]
    for half in range(2):
        columns = jnp.concatenate(
            [
                shifts[s][:, half * rows + r : half * rows + r + rows].reshape(-1, channels)
                for r in range(3)
                for s in range(3)
            ],
            axis=1,
        )
        pre = jnp.dot(columns, weight[...], preferred_element_type=jnp.float32)
        pre_all[half] = pre
        act_ref[half] = (pre * jax.nn.sigmoid(pre)).astype(jnp.bfloat16)
    pre_ref[...] = pre_all[lax.axis_index("tile")]


def split_kernel(arrived, near, _, mine_ref, other_ref, near_ref):
    tile = lax.axis_index("tile")
    near_ref[...] = near[...]
    mine_ref[...] = arrived[tile]
    other_ref[...] = arrived[1 - tile]


def forward_sum_kernel(partial, arrived, sum_ref):
    sum_ref[...] = (partial[...] + arrived[...].astype(jnp.float32)).astype(sum_ref.dtype)


def last_sum_kernel(keep, near, last, _, out_ref, *, scale):
    total = keep[...] + near[...].astype(jnp.float32) + last[...].astype(jnp.float32)
    out_ref[...] = total * scale


def transpose_kernel(own, other, out_ref, image):
    frames, rows, width, channels = own.shape
    tile = lax.axis_index("tile")
    whole_image(own, other, image)
    for which, first in enumerate((tile * rows, (1 - tile) * rows)):
        for r in range(3):
            block = image[:, pl.ds(first + r, rows)].reshape(-1, channels)
            out_ref[which, r * channels : (r + 1) * channels] = block.T


def slabs(own, first, second, ext):
    tile = lax.axis_index("tile")
    ext[2 * tile] = first[...]
    ext[1] = own[...]
    ext[2 - 2 * tile] = second[...]
    return ext[...].reshape(-1, own.shape[1])


def act_grad_kernel(own, first_in, second_in, weight, pre_ref, out_ref, ext):
    count, channels = own.shape
    frames = slabs(own, first_in, second_in, ext)
    hop = count // 4
    total = None
    for k in range(9):
        first = (8 - k) * hop
        term = lax.dot_general(
            frames[first : first + count],
            weight[k * channels : (k + 1) * channels],
            (((1,), (1,)), ((), ())),
            preferred_element_type=jnp.float32,
        )
        total = term if total is None else total + term
    act_grad = total.astype(jnp.bfloat16).astype(jnp.float32)
    pre = pre_ref[...]
    sig = jax.nn.sigmoid(pre)
    out_ref[...] = (act_grad * (sig * (1.0 + pre * (1.0 - sig)))).astype(jnp.bfloat16)


def temporal_kernel(feats, act, first_in, second_in, weight, out_ref, done_ref, ext):
    count, channels = feats.shape
    own = act.at[lax.axis_index("tile")]
    frames = slabs(own, first_in, second_in, ext)
    hop = count // 4
    columns = jnp.concatenate([frames[k * hop : k * hop + count] for k in range(9)], axis=1)
    mixed = jnp.dot(columns, weight[...], preferred_element_type=jnp.float32)
    out_ref[...] = (feats[...].astype(jnp.float32) + mixed).astype(jnp.bfloat16)
    done_ref[...] = jnp.zeros_like(done_ref)


def own_term_kernel(feats_t, own, total_ref):
    channels = own.shape[3]
    after, same, before = column_shifts(own[...].reshape(-1, channels), own.shape[2])
    left = feats_t[0]
    for s, right in enumerate((before, same, after)):
        total_ref[s] = jnp.dot(left, right, preferred_element_type=jnp.float32)


def kernel_grad_kernel(feats_t, other, term, far_ref, pass_ref, near_ref, keep_ref, total):
    frames, rows, width, channels = other.shape
    tile = lax.axis_index("tile")
    chip = lax.axis_index("frame")
    after, same, before = column_shifts(other[...].reshape(-1, channels), width)
    left = feats_t[1]
    for s, right in enumerate((before, same, after)):
        both = term[s] + jnp.dot(left, right, preferred_element_type=jnp.float32)
        for r in range(3):
            tap = 3 * r + s
            total[tap * channels : (tap + 1) * channels] = both[r * channels : (r + 1) * channels]
    share = keep_ref.shape[0]
    for distance, ref in ((3, far_ref), (2, pass_ref), (1, near_ref), (0, keep_ref)):
        first = (2 * (chip ^ distance) + tile) * share
        ref[...] = total[pl.ds(pl.multiple_of(first, 32), share)].astype(ref.dtype)


def input_grad_kernel(out_grad, own, other, weight, out_ref, ext):
    frames, rows, width, channels = own.shape
    with_edges(own, other, ext)
    after, same, before = column_shifts(ext[...].reshape(-1, channels), width)
    shifts = [piece.reshape(ext.shape) for piece in (before, same, after)]
    total = out_grad[...].astype(jnp.float32)
    for r in range(3):
        for s in range(3):
            tap = 3 * r + s
            total = total + lax.dot_general(
                shifts[s][:, 2 - r : 2 - r + rows].reshape(-1, channels),
                weight[tap * channels : (tap + 1) * channels],
                (((1,), (1,)), ((), ())),
                preferred_element_type=jnp.float32,
            )
    out_ref[...] = total.astype(jnp.bfloat16)


def per_device_pair(clip_feats, out_grad, spatial_weight, temporal_weight):
    frames, rows, width, channels = clip_feats.shape
    count = frames * rows * width
    chips = lax.axis_size("frame")
    cores = lax.axis_size("tile")
    scale = 1.0 / math.sqrt(frames * chips * rows * cores * width)
    outward = [(2 * z, 2 * z + 2) for z in range(chips - 1)]
    outward += [(2 * z + 3, 2 * z + 1) for z in range(chips - 1)]
    inward = [(target, source) for source, target in outward]
    both = ("frame", "tile")
    swap = [(0, 1), (1, 0)]
    bf16, f32 = jnp.bfloat16, jnp.float32
    product = 2 * count * 9 * channels * channels
    flat = (count, channels)
    ext = ((frames, rows + 2, width, channels), bf16)
    image = ((frames, 2 * rows + 2, width, channels), bf16)
    three = ((3, count, channels), bf16)

    grad_flat = out_grad.reshape(flat)
    feat_flat = clip_feats.reshape(flat)
    grad_first = lax.ppermute(grad_flat, both, outward)
    grad_second = lax.ppermute(grad_flat, both, inward)
    feat_other = lax.ppermute(clip_feats, "tile", swap)

    (first,) = kernel_call(first_kernel, [((8, 128), f32)], [], 5 * product)
    pre, act = kernel_call(
        spatial_kernel,
        [(flat, f32), ((2, *flat), bf16)],
        [image, ((2, *flat), f32)],
        2 * product,
        clip_feats, spatial_weight, feat_other, first, anywhere=1,
    )
    act_in = lax.ppermute(act, both, outward)
    (feats_t,) = kernel_call(
        transpose_kernel,
        [((2, 3 * channels, count), bf16)],
        [image],
        0,
        clip_feats, feat_other,
    )
    (pre_grad,) = kernel_call(
        act_grad_kernel,
        [(flat, bf16)],
        [three],
        product,
        grad_flat, grad_first, grad_second, temporal_weight, pre,
    )
    pre_grad = pre_grad.reshape(clip_feats.shape)
    pre_other = lax.ppermute(pre_grad, "tile", swap)

    share = (9 * channels // (chips * cores), channels)
    (term,) = kernel_call(
        own_term_kernel,
        [((3, 3 * channels, channels), f32)],
        [],
        product,
        feats_t, pre_grad,
    )
    far, onward, near, keep = kernel_call(
        kernel_grad_kernel,
        [(share, bf16), (share, f32), (share, bf16), (share, f32)],
        [((9 * channels, channels), f32)],
        product,
        feats_t, pre_other, term,
    )
    beside = [(z, z ^ 1) for z in range(chips)]
    across = [(z, z ^ 2) for z in range(chips)]
    far_in = lax.ppermute(far, "frame", beside)
    (onward,) = kernel_call(forward_sum_kernel, [(share, bf16)], [], 0, onward, far_in)
    last_in = lax.ppermute(onward, "frame", across)
    act_first, act_pass, near = kernel_call(
        split_kernel,
        [(flat, bf16), (flat, bf16), (share, bf16)],
        [],
        0,
        act_in, near, onward, anywhere=1,
    )
    near_in = lax.ppermute(near, "frame", beside)
    act_second = lax.ppermute(act_pass, "tile", swap)

    (input_grad,) = kernel_call(
        input_grad_kernel,
        [(flat, bf16)],
        [ext],
        product,
        grad_flat, pre_grad, pre_other, spatial_weight,
    )
    block_out, done = kernel_call(
        temporal_kernel,
        [(flat, bf16), ((8, 128), f32)],
        [three],
        product,
        feat_flat, act, act_first, act_second, temporal_weight,
    )
    (weight_grad,) = kernel_call(
        functools.partial(last_sum_kernel, scale=scale),
        [(share, f32)],
        [],
        0,
        keep, near_in, last_in, done, anywhere=1,
    )
    return (
        block_out.reshape(clip_feats.shape),
        input_grad.reshape(clip_feats.shape),
        weight_grad,
    )


def per_device(clip_feats, *rest):
    pairs = lax.axis_size("tile") == 2 and lax.axis_size("frame") == 4
    if pairs and clip_feats.shape[0] == 4 * TAP_DILATION:
        return per_device_pair(clip_feats, *rest)
    return per_device_any(clip_feats, *rest)


def solution(mesh):
    return jax.shard_map(
        per_device,
        mesh=mesh,
        in_specs=(
            P(("clip", "frame"), "tile", None, None),
            P(("clip", "frame"), "tile", None, None),
            P(),
            P(),
        ),
        out_specs=(
            P(("clip", "frame"), "tile", None, None),
            P(("clip", "frame"), "tile", None, None),
            P(("clip", "frame", "tile"), None),
        ),
        check_vma=False,
    )
```

profile of v0, /device:TPU:0, one launch (start us, length us, event | category | flops | bytes accessed | tf_op | source)
XLA Modules:
  0.0 36.4 jit_solution(17024730023642464802)
XLA Ops:
  0.6 0.0 copy-start.1
  0.6 0.0 copy-start.3
  0.6 5.1 %collective-permute-start.2 = (bf16[512,256]{1,0:T(8,128)(2,1)}, bf16[512,256]{1,0:T(8,128)(2,1)S(1)}, u32[]{:S(2)}, u32[]{:S(2)}) collective-permute-start(bf16[512,256]{1,0:T(8,128)(2,1)} %bitcast.9), channel_id=1, source_target_pairs={{0,2},{2,4},{4,6},{3,1},{5,3},{7,5},{8,10},{10,12},{12,14},{11,9},... | collective-permute-start | bytes 786440 | tf_op jit(solution)/shard_map/ppermute | solution.py:327
  5.7 1.3 %collective-permute-start.3 = (bf16[512,256]{1,0:T(8,128)(2,1)}, bf16[512,256]{1,0:T(8,128)(2,1)S(1)}, u32[]{:S(2)}, u32[]{:S(2)}) collective-permute-start(bf16[512,256]{1,0:T(8,128)(2,1)} %bitcast.10), channel_id=1, source_target_pairs={{2,0},{4,2},{6,4},{1,3},{3,5},{5,7},{10,8},{12,10},{14,12},{9,11},... | collective-permute-start | bytes 786440 | tf_op jit(solution)/shard_map/ppermute | solution.py:328
  7.0 0.3 collective-permute-start
  7.3 0.0 copy-start
  7.3 0.0 copy-start.2
  7.3 1.6 %collective-permute-done.other = bf16[8,4,16,256]{3,2,1,0:T(8,128)(2,1)S(1)} collective-permute-done((bf16[8,4,16,256]{3,2,1,0:T(8,128)(2,1)}, bf16[8,4,16,256]{3,2,1,0:T(8,128)(2,1)S(1)}, u32[]{:S(2)}, u32[]{:S(2)}) %collective-permute-start) | collective-permute-done | bytes 262176 | tf_op jit(solution)/shard_map/ppermute | solution.py:329
  8.8 0.0 copy-done.1
  8.8 0.0 copy-done.3
  8.9 1.7 %shard_map.68 = (f32[512,256]{1,0:T(8,128)S(1)}, bf16[2,512,256]{2,1,0:T(8,128)(2,1)S(1)}) custom-call(bf16[8,4,16,256]{3,2,1,0:T(8,128)(2,1)S(1)} %copy-done.1, bf16[2304,256]{1,0:T(8,128)(2,1)S(1)} %copy-done.3, bf16[8,4,16,256]{3,2,1,0:T(8,128)(2,1)S(1)} %collective-permute-done.other, f32[8,128]{1,0:T(8,128)S(1)} %shard_map.67._), custom_call_target="tpu_custom_call" | custom-call | flops 1207959552 | bytes 2756608 | tf_op jit(solution)/shard_map/pallas_call | solution.py:129
  10.6 4.6 %collective-permute-start.1 = (bf16[2,512,256]{2,1,0:T(8,128)(2,1)S(1)}, bf16[2,512,256]{2,1,0:T(8,128)(2,1)S(1)}, u32[]{:S(2)}, u32[]{:S(2)}) collective-permute-start(bf16[2,512,256]{2,1,0:T(8,128)(2,1)S(1)} %get-tuple-element.14.act), channel_id=1, source_target_pairs={{0,2},{2,4},{4,6},{3,1},{5,3},{7,5},{8,10},{10,12},{12,14},{11,9},... | collective-permute-start | bytes 1572872 | tf_op jit(solution)/shard_map/ppermute | solution.py:339
  15.2 0.0 collective-permute-done.2.first_in
  15.2 0.0 collective-permute-done.3.second_in
  15.2 0.0 copy-done
  15.2 0.0 copy-done.2
  15.2 0.8 %shard_map.70 = bf16[512,256]{1,0:T(8,128)(2,1)S(1)} custom-call(bf16[512,256]{1,0:T(8,128)(2,1)S(1)} %bitcast.11, bf16[512,256]{1,0:T(8,128)(2,1)S(1)} %collective-permute-done.2.first_in, bf16[512,256]{1,0:T(8,128)(2,1)S(1)} %collective-permute-done.3.second_in, bf16[2304,256]{1,0:T(8,128)(2,1)S(1)} %copy-done, f32[512,256]{1,0:T(8,128)S(1)} %get-tuple-element.15.pre_ref), custom_call_target="tpu_custom_call" | custom-call | flops 603979776 | bytes 2752512 | tf_op jit(solution)/shard_map/pallas_call | solution.py:129
  16.0 0.1 collective-permute-start.4
  16.1 0.5 %shard_map.69.feats_t = bf16[2,768,512]{2,1,0:T(8,128)(2,1)S(1)} custom-call(bf16[8,4,16,256]{3,2,1,0:T(8,128)(2,1)S(1)} %copy-done.1, bf16[8,4,16,256]{3,2,1,0:T(8,128)(2,1)S(1)} %collective-permute-done.other), custom_call_target="tpu_custom_call" | custom-call | bytes 2097152 | tf_op jit(solution)/shard_map/pallas_call | solution.py:129
  16.6 0.8 %shard_map.71.term = f32[3,768,256]{2,1,0:T(8,128)S(1)} custom-call(bf16[2,768,512]{2,1,0:T(8,128)(2,1)S(1)} %shard_map.69.feats_t, bf16[8,4,16,256]{3,2,1,0:T(8,128)(2,1)S(1)} %bitcast.7), custom_call_target="tpu_custom_call" | custom-call | flops 603979776 | bytes 4194304 | tf_op jit(solution)/shard_map/pallas_call | solution.py:129
  17.5 0.2 collective-permute-done.4.other
  17.6 0.9 %shard_map.72 = (bf16[288,256]{1,0:T(8,128)(2,1)S(1)}, f32[288,256]{1,0:T(8,128)S(1)}, bf16[288,256]{1,0:T(8,128)(2,1)S(1)}, f32[288,256]{1,0:T(8,128)S(1)}) custom-call(bf16[2,768,512]{2,1,0:T(8,128)(2,1)S(1)} %shard_map.69.feats_t, bf16[8,4,16,256]{3,2,1,0:T(8,128)(2,1)S(1)} %collective-permute-done.4.other, f32[3,768,256]{2,1,0:T(8,128)S(1)} %shard_map.71.term), custom_call_target="tpu_custom_call" | custom-call | flops 603979776 | bytes 5079040 | tf_op jit(solution)/shard_map/pallas_call | solution.py:129
  18.5 1.6 %collective-permute-start.5 = (bf16[288,256]{1,0:T(8,128)(2,1)S(1)}, bf16[288,256]{1,0:T(8,128)(2,1)S(1)}, u32[]{:S(2)}, u32[]{:S(2)}) collective-permute-start(bf16[288,256]{1,0:T(8,128)(2,1)S(1)} %get-tuple-element.18), channel_id=1, source_target_pairs={{0,2},{2,0},{4,6},{6,4},{1,3},{3,1},{5,7},{7,5},{8,10},{10,8},{12,... | collective-permute-start | bytes 442376 | tf_op jit(solution)/shard_map/ppermute | solution.py:374
  20.1 4.8 %collective-permute-done.5.arrived = bf16[288,256]{1,0:T(8,128)(2,1)S(1)} collective-permute-done((bf16[288,256]{1,0:T(8,128)(2,1)S(1)}, bf16[288,256]{1,0:T(8,128)(2,1)S(1)}, u32[]{:S(2)}, u32[]{:S(2)}) %collective-permute-start.5) | collective-permute-done | bytes 147488 | tf_op jit(solution)/shard_map/ppermute | solution.py:374
  25.0 0.0 collective-permute-done.1.arrived
  25.1 0.1 collective-permute-start.6
  25.2 2.7 %collective-permute-start.8 = (bf16[288,256]{1,0:T(8,128)(2,1)S(1)}, bf16[288,256]{1,0:T(8,128)(2,1)S(1)}, u32[]{:S(2)}, u32[]{:S(2)}) collective-permute-start(bf16[288,256]{1,0:T(8,128)(2,1)S(1)} %shard_map.73._), channel_id=1, source_target_pairs={{0,4},{2,6},{4,0},{6,2},{1,5},{3,7},{5,1},{7,3},{8,12},{10,14},{12... | collective-permute-start | bytes 442376 | tf_op jit(solution)/shard_map/ppermute | solution.py:376
  27.9 2.4 %collective-permute-start.7 = (bf16[288,256]{1,0:T(8,128)(2,1)S(1)}, bf16[288,256]{1,0:T(8,128)(2,1)S(1)}, u32[]{:S(2)}, u32[]{:S(2)}) collective-permute-start(bf16[288,256]{1,0:T(8,128)(2,1)S(1)} %get-tuple-element.23), channel_id=1, source_target_pairs={{0,2},{2,0},{4,6},{6,4},{1,3},{3,1},{5,7},{7,5},{8,10},{10,8},{12,... | collective-permute-start | bytes 442376 | tf_op jit(solution)/shard_map/ppermute | solution.py:384
  30.3 1.5 %shard_map.76 = bf16[512,256]{1,0:T(8,128)(2,1)} custom-call(bf16[512,256]{1,0:T(8,128)(2,1)S(1)} %bitcast.12, bf16[8,4,16,256]{3,2,1,0:T(8,128)(2,1)S(1)} %bitcast.8, bf16[8,4,16,256]{3,2,1,0:T(8,128)(2,1)S(1)} %collective-permute-done.4.other, bf16[2304,256]{1,0:T(8,128)(2,1)S(1)} %copy-done.3), custom_call_target="tpu_custom_call" | custom-call | flops 603979776 | bytes 2228224 | tf_op jit(solution)/shard_map/pallas_call | solution.py:129
  31.8 0.0 collective-permute-done.6.second_in
  31.8 1.5 %shard_map.75 = (bf16[512,256]{1,0:T(8,128)(2,1)}, f32[8,128]{1,0:T(8,128)S(1)}) custom-call(bf16[512,256]{1,0:T(8,128)(2,1)S(1)} %bitcast.5, bf16[2,512,256]{2,1,0:T(8,128)(2,1)S(1)} %get-tuple-element.14.act, bf16[512,256]{1,0:T(8,128)(2,1)S(1)} %get-tuple-element.19.first_in, bf16[512,256]{1,0:T(8,128)(2,1)S(1)} %collective-permute-done.6.second_in, ...), custom_call_target="tpu_custom_call" | custom-call | flops 603979776 | bytes 2756608 | tf_op jit(solution)/shard_map/pallas_call | solution.py:129
  33.3 2.3 %collective-permute-done.8.last = bf16[288,256]{1,0:T(8,128)(2,1)S(1)} collective-permute-done((bf16[288,256]{1,0:T(8,128)(2,1)S(1)}, bf16[288,256]{1,0:T(8,128)(2,1)S(1)}, u32[]{:S(2)}, u32[]{:S(2)}) %collective-permute-start.8) | collective-permute-done | bytes 147488 | tf_op jit(solution)/shard_map/ppermute | solution.py:376
  35.6 0.0 collective-permute-done.7.near
  35.6 0.8 %shard_map.77 = f32[288,256]{1,0:T(8,128)} custom-call(f32[288,256]{1,0:T(8,128)S(1)} %get-tuple-element.22.keep, bf16[288,256]{1,0:T(8,128)(2,1)S(1)} %collective-permute-done.7.near, bf16[288,256]{1,0:T(8,128)(2,1)S(1)} %collective-permute-done.8.last, f32[8,128]{1,0:T(8,128)S(1)} %get-tuple-element.24._), custom_call_target="tpu_custom_call" | custom-call | bytes 888832 | tf_op jit(solution)/shard_map/pallas_call | solution.py:129
  (3 shorter events, 0.1 us)
Async XLA Ops:
  0.6 8.2 %copy-start.1 = (bf16[8,4,16,256]{3,2,1,0:T(8,128)(2,1)S(1)}, bf16[8,4,16,256]{3,2,1,0:T(8,128)(2,1)}, u32[]{:S(2)}) copy-start(bf16[8,4,16,256]{3,2,1,0:T(8,128)(2,1)} %own.3) | copy-start | bytes 786436
  0.6 8.2 %copy-start.3 = (bf16[2304,256]{1,0:T(8,128)(2,1)S(1)}, bf16[2304,256]{1,0:T(8,128)(2,1)}, u32[]{:S(2)}) copy-start(bf16[2304,256]{1,0:T(8,128)(2,1)} %weight.7) | copy-start | bytes 3538948
  0.6 14.5 %collective-permute-start.2 = (bf16[512,256]{1,0:T(8,128)(2,1)}, bf16[512,256]{1,0:T(8,128)(2,1)S(1)}, u32[]{:S(2)}, u32[]{:S(2)}) collective-permute-start(bf16[512,256]{1,0:T(8,128)(2,1)} %bitcast.9), channel_id=1, source_target_pairs={{0,2},{2,4},{4,6},{3,1},{5,3},{7,5},{8,10},{10,12},{12,14},{11,9},... | collective-permute-start | bytes 786440 | tf_op jit(solution)/shard_map/ppermute | solution.py:327
  5.7 9.4 %collective-permute-start.3 = (bf16[512,256]{1,0:T(8,128)(2,1)}, bf16[512,256]{1,0:T(8,128)(2,1)S(1)}, u32[]{:S(2)}, u32[]{:S(2)}) collective-permute-start(bf16[512,256]{1,0:T(8,128)(2,1)} %bitcast.10), channel_id=1, source_target_pairs={{2,0},{4,2},{6,4},{1,3},{3,5},{5,7},{10,8},{12,10},{14,12},{9,11},... | collective-permute-start | bytes 786440 | tf_op jit(solution)/shard_map/ppermute | solution.py:328
  7.0 1.8 %collective-permute-start = (bf16[8,4,16,256]{3,2,1,0:T(8,128)(2,1)}, bf16[8,4,16,256]{3,2,1,0:T(8,128)(2,1)S(1)}, u32[]{:S(2)}, u32[]{:S(2)}) collective-permute-start(bf16[8,4,16,256]{3,2,1,0:T(8,128)(2,1)} %own.3), channel_id=1, source_target_pairs={{0,1},{1,0},{2,3},{3,2},{4,5},{5,4},{6,7},{7,6},{8,9},{9,8},{10,11... | collective-permute-start | bytes 786440 | tf_op jit(solution)/shard_map/ppermute | solution.py:329
  7.3 7.9 %copy-start = (bf16[2304,256]{1,0:T(8,128)(2,1)S(1)}, bf16[2304,256]{1,0:T(8,128)(2,1)}, u32[]{:S(2)}) copy-start(bf16[2304,256]{1,0:T(8,128)(2,1)} %weight.6) | copy-start | bytes 3538948
  7.3 7.9 %copy-start.2 = (bf16[8,4,16,256]{3,2,1,0:T(8,128)(2,1)S(1)}, bf16[8,4,16,256]{3,2,1,0:T(8,128)(2,1)}, u32[]{:S(2)}) copy-start(bf16[8,4,16,256]{3,2,1,0:T(8,128)(2,1)} %param.5) | copy-start | bytes 786436
  10.6 14.4 %collective-permute-start.1 = (bf16[2,512,256]{2,1,0:T(8,128)(2,1)S(1)}, bf16[2,512,256]{2,1,0:T(8,128)(2,1)S(1)}, u32[]{:S(2)}, u32[]{:S(2)}) collective-permute-start(bf16[2,512,256]{2,1,0:T(8,128)(2,1)S(1)} %get-tuple-element.14.act), channel_id=1, source_target_pairs={{0,2},{2,4},{4,6},{3,1},{5,3},{7,5},{8,10},{10,12},{12,14},{11,9},... | collective-permute-start | bytes 1572872 | tf_op jit(solution)/shard_map/ppermute | solution.py:339
  16.0 1.6 %collective-permute-start.4 = (bf16[8,4,16,256]{3,2,1,0:T(8,128)(2,1)S(1)}, bf16[8,4,16,256]{3,2,1,0:T(8,128)(2,1)S(1)}, u32[]{:S(2)}, u32[]{:S(2)}) collective-permute-start(bf16[8,4,16,256]{3,2,1,0:T(8,128)(2,1)S(1)} %bitcast.6), channel_id=1, source_target_pairs={{0,1},{1,0},{2,3},{3,2},{4,5},{5,4},{6,7},{7,6},{8,9},{9,8},{10,11... | collective-permute-start | bytes 786440 | tf_op jit(solution)/shard_map/ppermute | solution.py:355
  18.5 6.4 %collective-permute-start.5 = (bf16[288,256]{1,0:T(8,128)(2,1)S(1)}, bf16[288,256]{1,0:T(8,128)(2,1)S(1)}, u32[]{:S(2)}, u32[]{:S(2)}) collective-permute-start(bf16[288,256]{1,0:T(8,128)(2,1)S(1)} %get-tuple-element.18), channel_id=1, source_target_pairs={{0,2},{2,0},{4,6},{6,4},{1,3},{3,1},{5,7},{7,5},{8,10},{10,8},{12,... | collective-permute-start | bytes 442376 | tf_op jit(solution)/shard_map/ppermute | solution.py:374
  25.1 6.8 %collective-permute-start.6 = (bf16[512,256]{1,0:T(8,128)(2,1)S(1)}, bf16[512,256]{1,0:T(8,128)(2,1)S(1)}, u32[]{:S(2)}, u32[]{:S(2)}) collective-permute-start(bf16[512,256]{1,0:T(8,128)(2,1)S(1)} %get-tuple-element.20), channel_id=1, source_target_pairs={{0,1},{1,0},{2,3},{3,2},{4,5},{5,4},{6,7},{7,6},{8,9},{9,8},{10,11... | collective-permute-start | bytes 786440 | tf_op jit(solution)/shard_map/ppermute | solution.py:385
  25.2 10.4 %collective-permute-start.8 = (bf16[288,256]{1,0:T(8,128)(2,1)S(1)}, bf16[288,256]{1,0:T(8,128)(2,1)S(1)}, u32[]{:S(2)}, u32[]{:S(2)}) collective-permute-start(bf16[288,256]{1,0:T(8,128)(2,1)S(1)} %shard_map.73._), channel_id=1, source_target_pairs={{0,4},{2,6},{4,0},{6,2},{1,5},{3,7},{5,1},{7,3},{8,12},{10,14},{12... | collective-permute-start | bytes 442376 | tf_op jit(solution)/shard_map/ppermute | solution.py:376
  27.9 7.7 %collective-permute-start.7 = (bf16[288,256]{1,0:T(8,128)(2,1)S(1)}, bf16[288,256]{1,0:T(8,128)(2,1)S(1)}, u32[]{:S(2)}, u32[]{:S(2)}) collective-permute-start(bf16[288,256]{1,0:T(8,128)(2,1)S(1)} %get-tuple-element.23), channel_id=1, source_target_pairs={{0,2},{2,0},{4,6},{6,4},{1,3},{3,1},{5,7},{7,5},{8,10},{10,8},{12,... | collective-permute-start | bytes 442376 | tf_op jit(solution)/shard_map/ppermute | solution.py:384
where the time goes:
time: 36.6 us; the launch traced here: 36.4 us
  starting transfers between devices  18.1 us (49%)
  waiting for transfers between devices  8.85 us (24%)
  Pallas kernels  8.66 us (24%)
  between operations  0.78 us (2%)
    pallas_call x11, Pallas kernels, kernel_call(): pl.pallas_call(body, out_shape=tuple((jax.ShapeDtypeStruct(shape, kind) f...  8.66 us
    ppermute x1, starting transfers between devices, per_device_pair(): grad_first = lax.ppermute(grad_flat, both, outward)  5.08 us
    ppermute x1, waiting for transfers between devices, per_device_pair(): far_in = lax.ppermute(far, 'frame', beside)  4.83 us
    ppermute x1, starting transfers between devices, per_device_pair(): act_in = lax.ppermute(act, both, outward)  4.58 us
    ppermute x1, starting transfers between devices, per_device_pair(): last_in = lax.ppermute(onward, 'frame', across)  2.73 us
    ppermute x1, starting transfers between devices, per_device_pair(): near_in = lax.ppermute(near, 'frame', beside)  2.4 us
    ppermute x1, waiting for transfers between devices, per_device_pair(): last_in = lax.ppermute(onward, 'frame', across)  2.25 us
    ppermute x1, starting transfers between devices, per_device_pair(): far_in = lax.ppermute(far, 'frame', beside)  1.6 us
  transfers between devices with their start and end apart: 9, of which 4 were waited for; matrix products, arithmetic and copies ran while one was open for 0% of the time, Pallas kernels for 22%

commit v1 on v0

--- a/solution.py
+++ b/solution.py
@@ -203,13 +203,17 @@
     other_ref[...] = arrived[1 - tile]
 
 
-def forward_sum_kernel(partial, arrived, sum_ref):
-    sum_ref[...] = (partial[...] + arrived[...].astype(jnp.float32)).astype(sum_ref.dtype)
-
-
-def last_sum_kernel(keep, near, last, _, out_ref, *, scale):
-    total = keep[...] + near[...].astype(jnp.float32) + last[...].astype(jnp.float32)
-    out_ref[...] = total * scale
+def forward_sum_kernel(partial, arrived, *rest, first):
+    sum_ref = rest[-1]
+    rows = partial[first : first + sum_ref.shape[0]]
+    sum_ref[...] = (rows + arrived[...].astype(jnp.float32)).astype(sum_ref.dtype)
+
+
+def last_sum_kernel(keep, near, last_a, last_b, _, out_ref, *, scale):
+    half = last_a.shape[0]
+    for first, last in ((0, last_a), (half, last_b)):
+        total = keep[first : first + half] + near[first : first + half].astype(jnp.float32)
+        out_ref[first : first + half] = (total + last[...].astype(jnp.float32)) * scale
 
 
 def transpose_kernel(own, other, out_ref, image):
@@ -269,7 +273,9 @@
         total_ref[s] = jnp.dot(left, right, preferred_element_type=jnp.float32)
 
 
-def kernel_grad_kernel(feats_t, other, term, far_ref, pass_ref, near_ref, keep_ref, total):
+def kernel_grad_kernel(
+    feats_t, other, term, far_a_ref, far_b_ref, pass_ref, near_ref, keep_ref, total
+):
     frames, rows, width, channels = other.shape
     tile = lax.axis_index("tile")
     chip = lax.axis_index("frame")
@@ -281,12 +287,19 @@
             tap = 3 * r + s
             total[tap * channels : (tap + 1) * channels] = both[r * channels : (r + 1) * channels]
     share = keep_ref.shape[0]
-    for distance, ref in ((3, far_ref), (2, pass_ref), (1, near_ref), (0, keep_ref)):
-        first = (2 * (chip ^ distance) + tile) * share
-        ref[...] = total[pl.ds(pl.multiple_of(first, 32), share)].astype(ref.dtype)
-
-
-def input_grad_kernel(out_grad, own, other, weight, out_ref, ext):
+    half = share // 2
+    for distance, skip, ref in (
+        (3, 0, far_a_ref),
+        (3, half, far_b_ref),
+        (2, 0, pass_ref),
+        (1, 0, near_ref),
+        (0, 0, keep_ref),
+    ):
+        first = (2 * (chip ^ distance) + tile) * share + skip
+        ref[...] = total[pl.ds(pl.multiple_of(first, 16), ref.shape[0])].astype(ref.dtype)
+
+
+def input_grad_kernel(out_grad, own, other, weight, _, out_ref, ext):
     frames, rows, width, channels = own.shape
     with_edges(own, other, ext)
     after, same, before = column_shifts(ext[...].reshape(-1, channels), width)
@@ -328,7 +341,7 @@
     grad_second = lax.ppermute(grad_flat, both, inward)
     feat_other = lax.ppermute(clip_feats, "tile", swap)
 
-    (first,) = kernel_call(first_kernel, [((8, 128), f32)], [], 5 * product)
+    (first,) = kernel_call(first_kernel, [((8, 128), f32)], [], 2 * product)
     pre, act = kernel_call(
         spatial_kernel,
         [(flat, f32), ((2, *flat), bf16)],
@@ -362,24 +375,36 @@
         product,
         feats_t, pre_grad,
     )
-    far, onward, near, keep = kernel_call(
+    half = (share[0] // 2, channels)
+    far_a, far_b, onward, near, keep = kernel_call(
         kernel_grad_kernel,
-        [(share, bf16), (share, f32), (share, bf16), (share, f32)],
+        [(half, bf16), (half, bf16), (share, f32), (share, bf16), (share, f32)],
         [((9 * channels, channels), f32)],
         product,
         feats_t, pre_other, term,
     )
     beside = [(z, z ^ 1) for z in range(chips)]
     across = [(z, z ^ 2) for z in range(chips)]
-    far_in = lax.ppermute(far, "frame", beside)
-    (onward,) = kernel_call(forward_sum_kernel, [(share, bf16)], [], 0, onward, far_in)
-    last_in = lax.ppermute(onward, "frame", across)
+    far_in_a = lax.ppermute(far_a, "frame", beside)
+    far_in_b = lax.ppermute(far_b, "frame", beside)
+    (sum_a,) = kernel_call(
+        functools.partial(forward_sum_kernel, first=0), [(half, bf16)], [], 0, onward, far_in_a
+    )
+    last_a = lax.ppermute(sum_a, "frame", across)
+    (sum_b,) = kernel_call(
+        functools.partial(forward_sum_kernel, first=half[0]),
+        [(half, bf16)],
+        [],
+        0,
+        onward, far_in_b, sum_a, anywhere=1,
+    )
+    last_b = lax.ppermute(sum_b, "frame", across)
     act_first, act_pass, near = kernel_call(
         split_kernel,
         [(flat, bf16), (flat, bf16), (share, bf16)],
         [],
         0,
-        act_in, near, onward, anywhere=1,
+        act_in, near, sum_b, anywhere=1,
     )
     near_in = lax.ppermute(near, "frame", beside)
     act_second = lax.ppermute(act_pass, "tile", swap)
@@ -388,8 +413,8 @@
         input_grad_kernel,
         [(flat, bf16)],
         [ext],
-        product,
-        grad_flat, pre_grad, pre_other, spatial_weight,
+        20 * product,
+        grad_flat, pre_grad, pre_other, spatial_weight, last_a, anywhere=1,
     )
     block_out, done = kernel_call(
         temporal_kernel,
@@ -403,7 +428,7 @@
         [(share, f32)],
         [],
         0,
-        keep, near_in, last_in, done, anywhere=1,
+        keep, near_in, last_a, last_b, done, anywhere=1,
     )
     return (
         block_out.reshape(clip_feats.shape),

time: 36.6 us -> 35.6 us (0.973)
  waiting for transfers between devices: 8.85 us -> 6.66 us
  starting transfers between devices: 18.1 us -> 19.2 us
    ppermute x2 -> x4, waiting for transfers between devices: 7.09 us -> 5.14 us  [the longest x1 2.84 us: per_device_pair(): far_in_a = lax.ppermute(far_a, 'frame', beside)]
    ppermute x2 -> x4, starting transfers between devices: 4.33 us -> 5.94 us  [the longest x1 2.87 us: per_device_pair(): last_a = lax.ppermute(sum_a, 'frame', across)]
    ppermute x1, waiting for transfers between devices: 1.55 us -> 0.01 us  [per_device_pair(): feat_other = lax.ppermute(clip_feats, 'tile', swap)]
    ppermute x1, waiting for transfers between devices: 0.01 us -> 0.78 us  [per_device_pair(): grad_second = lax.ppermute(grad_flat, both, inward)]
    ppermute x1, waiting for transfers between devices: 0.02 us -> 0.56 us  [per_device_pair(): near_in = lax.ppermute(near, 'frame', beside)]
    ppermute x1, starting transfers between devices: 5.08 us -> 4.65 us  [per_device_pair(): grad_first = lax.ppermute(grad_flat, both, outward)]
    pallas_call x11 -> x12, Pallas kernels: 8.66 us -> 8.7 us  [kernel_call(): pl.pallas_call(body, out_shape=tuple((jax.ShapeDtypeStruct(shape, kind) f...]
  transfers between devices with their start and end apart: 9 -> 11, of which waited for: 4 -> 5; matrix products, arithmetic and copies ran while one was open for 0% -> 0% of each run, Pallas kernels for 22% -> 22%
where the time goes in v1:
time: 35.6 us; the launch traced here: 35.4 us
  starting transfers between devices  19.2 us (54%)
  Pallas kernels  8.7 us (24%)
  waiting for transfers between devices  6.66 us (19%)
  between operations  0.78 us (2%)
    pallas_call x12, Pallas kernels, kernel_call(): pl.pallas_call(body, out_shape=tuple((jax.ShapeDtypeStruct(shape, kind) f...  8.7 us
    ppermute x1, starting transfers between devices, per_device_pair(): grad_first = lax.ppermute(grad_flat, both, outward)  4.65 us
    ppermute x1, starting transfers between devices, per_device_pair(): act_in = lax.ppermute(act, both, outward)  4.58 us
    ppermute x1, starting transfers between devices, per_device_pair(): last_a = lax.ppermute(sum_a, 'frame', across)  2.87 us
    ppermute x1, waiting for transfers between devices, per_device_pair(): far_in_a = lax.ppermute(far_a, 'frame', beside)  2.84 us
    ppermute x1, waiting for transfers between devices, per_device_pair(): last_a = lax.ppermute(sum_a, 'frame', across)  2.3 us
    ppermute x1, starting transfers between devices, per_device_pair(): near_in = lax.ppermute(near, 'frame', beside)  2.08 us
    ppermute x1, starting transfers between devices, per_device_pair(): far_in_a = lax.ppermute(far_a, 'frame', beside)  1.63 us
  transfers between devices with their start and end apart: 11, of which 5 were waited for; matrix products, arithmetic and copies ran while one was open for 0% of the time, Pallas kernels for 22%

profile of v1, /device:TPU:0, one launch (start us, length us, event | category | flops | bytes accessed | tf_op | source)
XLA Modules:
  0.0 35.4 jit_solution(17818998491086767181)
XLA Ops:
  0.6 0.5 %collective-permute-start = (bf16[8,4,16,256]{3,2,1,0:T(8,128)(2,1)}, bf16[8,4,16,256]{3,2,1,0:T(8,128)(2,1)S(1)}, u32[]{:S(2)}, u32[]{:S(2)}) collective-permute-start(bf16[8,4,16,256]{3,2,1,0:T(8,128)(2,1)} %own.3), channel_id=1, source_target_pairs={{0,1},{1,0},{2,3},{3,2},{4,5},{5,4},{6,7},{7,6},{8,9},{9,8},{10,11... | collective-permute-start | bytes 786440 | tf_op jit(solution)/shard_map/ppermute | solution.py:342
  1.1 0.0 copy-start.1
  1.1 0.0 copy-start.3
  1.2 4.7 %collective-permute-start.2 = (bf16[512,256]{1,0:T(8,128)(2,1)}, bf16[512,256]{1,0:T(8,128)(2,1)S(1)}, u32[]{:S(2)}, u32[]{:S(2)}) collective-permute-start(bf16[512,256]{1,0:T(8,128)(2,1)} %bitcast.9), channel_id=1, source_target_pairs={{0,2},{2,4},{4,6},{3,1},{5,3},{7,5},{8,10},{10,12},{12,14},{11,9},... | collective-permute-start | bytes 786440 | tf_op jit(solution)/shard_map/ppermute | solution.py:340
  5.8 1.3 %collective-permute-start.3 = (bf16[512,256]{1,0:T(8,128)(2,1)}, bf16[512,256]{1,0:T(8,128)(2,1)S(1)}, u32[]{:S(2)}, u32[]{:S(2)}) collective-permute-start(bf16[512,256]{1,0:T(8,128)(2,1)} %bitcast.10), channel_id=1, source_target_pairs={{2,0},{4,2},{6,4},{1,3},{3,5},{5,7},{10,8},{12,10},{14,12},{9,11},... | collective-permute-start | bytes 786440 | tf_op jit(solution)/shard_map/ppermute | solution.py:341
  7.1 0.0 copy-start
  7.1 0.0 copy-start.2
  7.1 0.0 collective-permute-done.other
  7.2 0.0 copy-done.1
  7.2 0.0 copy-done.3
  7.2 1.7 %shard_map.68 = (f32[512,256]{1,0:T(8,128)S(1)}, bf16[2,512,256]{2,1,0:T(8,128)(2,1)S(1)}) custom-call(bf16[8,4,16,256]{3,2,1,0:T(8,128)(2,1)S(1)} %copy-done.1, bf16[2304,256]{1,0:T(8,128)(2,1)S(1)} %copy-done.3, bf16[8,4,16,256]{3,2,1,0:T(8,128)(2,1)S(1)} %collective-permute-done.other, f32[8,128]{1,0:T(8,128)S(1)} %shard_map.67._), custom_call_target="tpu_custom_call" | custom-call | flops 1207959552 | bytes 2756608 | tf_op jit(solution)/shard_map/pallas_call | solution.py:129
  8.9 4.6 %collective-permute-start.1 = (bf16[2,512,256]{2,1,0:T(8,128)(2,1)S(1)}, bf16[2,512,256]{2,1,0:T(8,128)(2,1)S(1)}, u32[]{:S(2)}, u32[]{:S(2)}) collective-permute-start(bf16[2,512,256]{2,1,0:T(8,128)(2,1)S(1)} %get-tuple-element.15.act), channel_id=1, source_target_pairs={{0,2},{2,4},{4,6},{3,1},{5,3},{7,5},{8,10},{10,12},{12,14},{11,9},... | collective-permute-start | bytes 1572872 | tf_op jit(solution)/shard_map/ppermute | solution.py:352
  13.5 0.0 collective-permute-done.2.first_in
  13.5 0.8 %collective-permute-done.3.second_in = bf16[512,256]{1,0:T(8,128)(2,1)S(1)} collective-permute-done((bf16[512,256]{1,0:T(8,128)(2,1)}, bf16[512,256]{1,0:T(8,128)(2,1)S(1)}, u32[]{:S(2)}, u32[]{:S(2)}) %collective-permute-start.3) | collective-permute-done | bytes 262176 | tf_op jit(solution)/shard_map/ppermute | solution.py:341
  14.3 0.0 copy-done
  14.3 0.0 copy-done.2
  14.3 0.8 %shard_map.70 = bf16[512,256]{1,0:T(8,128)(2,1)S(1)} custom-call(bf16[512,256]{1,0:T(8,128)(2,1)S(1)} %bitcast.11, bf16[512,256]{1,0:T(8,128)(2,1)S(1)} %collective-permute-done.2.first_in, bf16[512,256]{1,0:T(8,128)(2,1)S(1)} %collective-permute-done.3.second_in, bf16[2304,256]{1,0:T(8,128)(2,1)S(1)} %copy-done, f32[512,256]{1,0:T(8,128)S(1)} %get-tuple-element.16.pre_ref), custom_call_target="tpu_custom_call" | custom-call | flops 603979776 | bytes 2752512 | tf_op jit(solution)/shard_map/pallas_call | solution.py:129
  15.1 0.1 collective-permute-start.4
  15.2 0.5 %shard_map.69.feats_t = bf16[2,768,512]{2,1,0:T(8,128)(2,1)S(1)} custom-call(bf16[8,4,16,256]{3,2,1,0:T(8,128)(2,1)S(1)} %copy-done.1, bf16[8,4,16,256]{3,2,1,0:T(8,128)(2,1)S(1)} %collective-permute-done.other), custom_call_target="tpu_custom_call" | custom-call | bytes 2097152 | tf_op jit(solution)/shard_map/pallas_call | solution.py:129
  15.7 0.8 %shard_map.71.term = f32[3,768,256]{2,1,0:T(8,128)S(1)} custom-call(bf16[2,768,512]{2,1,0:T(8,128)(2,1)S(1)} %shard_map.69.feats_t, bf16[8,4,16,256]{3,2,1,0:T(8,128)(2,1)S(1)} %bitcast.7), custom_call_target="tpu_custom_call" | custom-call | flops 603979776 | bytes 4194304 | tf_op jit(solution)/shard_map/pallas_call | solution.py:129
  16.6 0.2 collective-permute-done.4.other
  16.7 0.9 %shard_map.72 = (bf16[144,256]{1,0:T(8,128)(2,1)S(1)}, bf16[144,256]{1,0:T(8,128)(2,1)S(1)}, f32[288,256]{1,0:T(8,128)S(1)}, bf16[288,256]{1,0:T(8,128)(2,1)S(1)}, f32[288,256]{1,0:T(8,128)S(1)}) custom-call(bf16[2,768,512]{2,1,0:T(8,128)(2,1)S(1)} %shard_map.69.feats_t, bf16[8,4,16,256]{3,2,1,0:T(8,128)(2,1)S(1)} %collective-permute-done.4.other, ...), custom_call_target="tpu_custom_call" | custom-call | flops 603979776 | bytes 5079040 | tf_op jit(solution)/shard_map/pallas_call | solution.py:129
  17.6 1.6 %collective-permute-start.6 = (bf16[144,256]{1,0:T(8,128)(2,1)S(1)}, bf16[144,256]{1,0:T(8,128)(2,1)S(1)}, u32[]{:S(2)}, u32[]{:S(2)}) collective-permute-start(bf16[144,256]{1,0:T(8,128)(2,1)S(1)} %get-tuple-element.20), channel_id=1, source_target_pairs={{0,2},{2,0},{4,6},{6,4},{1,3},{3,1},{5,7},{7,5},{8,10},{10,8},{12,... | collective-permute-start | bytes 221192 | tf_op jit(solution)/shard_map/ppermute | solution.py:388
  19.3 0.5 %collective-permute-start.5 = (bf16[144,256]{1,0:T(8,128)(2,1)S(1)}, bf16[144,256]{1,0:T(8,128)(2,1)S(1)}, u32[]{:S(2)}, u32[]{:S(2)}) collective-permute-start(bf16[144,256]{1,0:T(8,128)(2,1)S(1)} %get-tuple-element.19), channel_id=1, source_target_pairs={{0,2},{2,0},{4,6},{6,4},{1,3},{3,1},{5,7},{7,5},{8,10},{10,8},{12,... | collective-permute-start | bytes 221192 | tf_op jit(solution)/shard_map/ppermute | solution.py:389
  19.7 2.8 %collective-permute-done.6.arrived = bf16[144,256]{1,0:T(8,128)(2,1)S(1)} collective-permute-done((bf16[144,256]{1,0:T(8,128)(2,1)S(1)}, bf16[144,256]{1,0:T(8,128)(2,1)S(1)}, u32[]{:S(2)}, u32[]{:S(2)}) %collective-permute-start.6) | collective-permute-done | bytes 73760 | tf_op jit(solution)/shard_map/ppermute | solution.py:388
  22.6 2.9 %collective-permute-start.8 = (bf16[144,256]{1,0:T(8,128)(2,1)S(1)}, bf16[144,256]{1,0:T(8,128)(2,1)S(1)}, u32[]{:S(2)}, u32[]{:S(2)}) collective-permute-start(bf16[144,256]{1,0:T(8,128)(2,1)S(1)} %shard_map.73.rest_0_), channel_id=1, source_target_pairs={{0,4},{2,6},{4,0},{6,2},{1,5},{3,7},{5,1},{7,3},{8,12},{10,14},{12... | collective-permute-start | bytes 221192 | tf_op jit(solution)/shard_map/ppermute | solution.py:393
  25.4 0.0 collective-permute-done.5.arrived
  25.5 1.0 %collective-permute-start.10 = (bf16[144,256]{1,0:T(8,128)(2,1)S(1)}, bf16[144,256]{1,0:T(8,128)(2,1)S(1)}, u32[]{:S(2)}, u32[]{:S(2)}) collective-permute-start(bf16[144,256]{1,0:T(8,128)(2,1)S(1)} %shard_map.74._), channel_id=1, source_target_pairs={{0,4},{2,6},{4,0},{6,2},{1,5},{3,7},{5,1},{7,3},{8,12},{10,14},{12... | collective-permute-start | bytes 221192 | tf_op jit(solution)/shard_map/ppermute | solution.py:401
  26.5 0.0 collective-permute-done.1.arrived
  26.5 0.1 collective-permute-start.7
  26.6 2.1 %collective-permute-start.9 = (bf16[288,256]{1,0:T(8,128)(2,1)S(1)}, bf16[288,256]{1,0:T(8,128)(2,1)S(1)}, u32[]{:S(2)}, u32[]{:S(2)}) collective-permute-start(bf16[288,256]{1,0:T(8,128)(2,1)S(1)} %get-tuple-element.25), channel_id=1, source_target_pairs={{0,2},{2,0},{4,6},{6,4},{1,3},{3,1},{5,7},{7,5},{8,10},{10,8},{12,... | collective-permute-start | bytes 442376 | tf_op jit(solution)/shard_map/ppermute | solution.py:409
  28.7 2.3 %collective-permute-done.8._.last_a = bf16[144,256]{1,0:T(8,128)(2,1)S(1)} collective-permute-done((bf16[144,256]{1,0:T(8,128)(2,1)S(1)}, bf16[144,256]{1,0:T(8,128)(2,1)S(1)}, u32[]{:S(2)}, u32[]{:S(2)}) %collective-permute-start.8) | collective-permute-done | bytes 73760 | tf_op jit(solution)/shard_map/ppermute | solution.py:393
  31.0 1.5 %shard_map.77 = bf16[512,256]{1,0:T(8,128)(2,1)} custom-call(bf16[512,256]{1,0:T(8,128)(2,1)S(1)} %bitcast.12, bf16[8,4,16,256]{3,2,1,0:T(8,128)(2,1)S(1)} %bitcast.8, bf16[8,4,16,256]{3,2,1,0:T(8,128)(2,1)S(1)} %collective-permute-done.4.other, bf16[2304,256]{1,0:T(8,128)(2,1)S(1)} %copy-done.3, bf16[144,256]{1,0:T(8,128)(2,1)S(1)} %collective-permute-done.8._.last_a), custom_call_target="tpu_custom_call" | custom-call | flops 12079595520 | bytes 2301952 | tf_op jit(solution)/shard_map/pallas_call | solution.py:129
  32.5 0.0 collective-permute-done.7.second_in
  32.5 1.5 %shard_map.76 = (bf16[512,256]{1,0:T(8,128)(2,1)}, f32[8,128]{1,0:T(8,128)S(1)}) custom-call(bf16[512,256]{1,0:T(8,128)(2,1)S(1)} %bitcast.5, bf16[2,512,256]{2,1,0:T(8,128)(2,1)S(1)} %get-tuple-element.15.act, bf16[512,256]{1,0:T(8,128)(2,1)S(1)} %get-tuple-element.21.first_in, bf16[512,256]{1,0:T(8,128)(2,1)S(1)} %collective-permute-done.7.second_in, ...), custom_call_target="tpu_custom_call" | custom-call | flops 603979776 | bytes 2756608 | tf_op jit(solution)/shard_map/pallas_call | solution.py:129
  34.0 0.0 collective-permute-done.10.last_b
  34.0 0.6 %collective-permute-done.9.near = bf16[288,256]{1,0:T(8,128)(2,1)S(1)} collective-permute-done((bf16[288,256]{1,0:T(8,128)(2,1)S(1)}, bf16[288,256]{1,0:T(8,128)(2,1)S(1)}, u32[]{:S(2)}, u32[]{:S(2)}) %collective-permute-start.9) | collective-permute-done | bytes 147488 | tf_op jit(solution)/shard_map/ppermute | solution.py:409
  34.6 0.8 %shard_map.78 = f32[288,256]{1,0:T(8,128)} custom-call(f32[288,256]{1,0:T(8,128)S(1)} %get-tuple-element.24.keep, bf16[288,256]{1,0:T(8,128)(2,1)S(1)} %collective-permute-done.9.near, bf16[144,256]{1,0:T(8,128)(2,1)S(1)} %collective-permute-done.8._.last_a, bf16[144,256]{1,0:T(8,128)(2,1)S(1)} %collective-permute-done.10.last_b, ...), custom_call_target="tpu_custom_call" | custom-call | bytes 888832 | tf_op jit(solution)/shard_map/pallas_call | solution.py:129
  (4 shorter events, 0.1 us)
Async XLA Ops:
  0.6 6.5 %collective-permute-start = (bf16[8,4,16,256]{3,2,1,0:T(8,128)(2,1)}, bf16[8,4,16,256]{3,2,1,0:T(8,128)(2,1)S(1)}, u32[]{:S(2)}, u32[]{:S(2)}) collective-permute-start(bf16[8,4,16,256]{3,2,1,0:T(8,128)(2,1)} %own.3), channel_id=1, source_target_pairs={{0,1},{1,0},{2,3},{3,2},{4,5},{5,4},{6,7},{7,6},{8,9},{9,8},{10,11... | collective-permute-start | bytes 786440 | tf_op jit(solution)/shard_map/ppermute | solution.py:342
  1.1 6.0 %copy-start.1 = (bf16[8,4,16,256]{3,2,1,0:T(8,128)(2,1)S(1)}, bf16[8,4,16,256]{3,2,1,0:T(8,128)(2,1)}, u32[]{:S(2)}) copy-start(bf16[8,4,16,256]{3,2,1,0:T(8,128)(2,1)} %own.3) | copy-start | bytes 786436
  1.1 6.0 %copy-start.3 = (bf16[2304,256]{1,0:T(8,128)(2,1)S(1)}, bf16[2304,256]{1,0:T(8,128)(2,1)}, u32[]{:S(2)}) copy-start(bf16[2304,256]{1,0:T(8,128)(2,1)} %weight.7) | copy-start | bytes 3538948
  1.2 12.4 %collective-permute-start.2 = (bf16[512,256]{1,0:T(8,128)(2,1)}, bf16[512,256]{1,0:T(8,128)(2,1)S(1)}, u32[]{:S(2)}, u32[]{:S(2)}) collective-permute-start(bf16[512,256]{1,0:T(8,128)(2,1)} %bitcast.9), channel_id=1, source_target_pairs={{0,2},{2,4},{4,6},{3,1},{5,3},{7,5},{8,10},{10,12},{12,14},{11,9},... | collective-permute-start | bytes 786440 | tf_op jit(solution)/shard_map/ppermute | solution.py:340
  5.8 8.5 %collective-permute-start.3 = (bf16[512,256]{1,0:T(8,128)(2,1)}, bf16[512,256]{1,0:T(8,128)(2,1)S(1)}, u32[]{:S(2)}, u32[]{:S(2)}) collective-permute-start(bf16[512,256]{1,0:T(8,128)(2,1)} %bitcast.10), channel_id=1, source_target_pairs={{2,0},{4,2},{6,4},{1,3},{3,5},{5,7},{10,8},{12,10},{14,12},{9,11},... | collective-permute-start | bytes 786440 | tf_op jit(solution)/shard_map/ppermute | solution.py:341
  7.1 7.2 %copy-start = (bf16[2304,256]{1,0:T(8,128)(2,1)S(1)}, bf16[2304,256]{1,0:T(8,128)(2,1)}, u32[]{:S(2)}) copy-start(bf16[2304,256]{1,0:T(8,128)(2,1)} %weight.6) | copy-start | bytes 3538948
  7.1 7.2 %copy-start.2 = (bf16[8,4,16,256]{3,2,1,0:T(8,128)(2,1)S(1)}, bf16[8,4,16,256]{3,2,1,0:T(8,128)(2,1)}, u32[]{:S(2)}) copy-start(bf16[8,4,16,256]{3,2,1,0:T(8,128)(2,1)} %param.5) | copy-start | bytes 786436
  8.9 17.5 %collective-permute-start.1 = (bf16[2,512,256]{2,1,0:T(8,128)(2,1)S(1)}, bf16[2,512,256]{2,1,0:T(8,128)(2,1)S(1)}, u32[]{:S(2)}, u32[]{:S(2)}) collective-permute-start(bf16[2,512,256]{2,1,0:T(8,128)(2,1)S(1)} %get-tuple-element.15.act), channel_id=1, source_target_pairs={{0,2},{2,4},{4,6},{3,1},{5,3},{7,5},{8,10},{10,12},{12,14},{11,9},... | collective-permute-start | bytes 1572872 | tf_op jit(solution)/shard_map/ppermute | solution.py:352
  15.1 1.6 %collective-permute-start.4 = (bf16[8,4,16,256]{3,2,1,0:T(8,128)(2,1)S(1)}, bf16[8,4,16,256]{3,2,1,0:T(8,128)(2,1)S(1)}, u32[]{:S(2)}, u32[]{:S(2)}) collective-permute-start(bf16[8,4,16,256]{3,2,1,0:T(8,128)(2,1)S(1)} %bitcast.6), channel_id=1, source_target_pairs={{0,1},{1,0},{2,3},{3,2},{4,5},{5,4},{6,7},{7,6},{8,9},{9,8},{10,11... | collective-permute-start | bytes 786440 | tf_op jit(solution)/shard_map/ppermute | solution.py:368
  17.6 4.9 %collective-permute-start.6 = (bf16[144,256]{1,0:T(8,128)(2,1)S(1)}, bf16[144,256]{1,0:T(8,128)(2,1)S(1)}, u32[]{:S(2)}, u32[]{:S(2)}) collective-permute-start(bf16[144,256]{1,0:T(8,128)(2,1)S(1)} %get-tuple-element.20), channel_id=1, source_target_pairs={{0,2},{2,0},{4,6},{6,4},{1,3},{3,1},{5,7},{7,5},{8,10},{10,8},{12,... | collective-permute-start | bytes 221192 | tf_op jit(solution)/shard_map/ppermute | solution.py:388
  19.3 6.2 %collective-permute-start.5 = (bf16[144,256]{1,0:T(8,128)(2,1)S(1)}, bf16[144,256]{1,0:T(8,128)(2,1)S(1)}, u32[]{:S(2)}, u32[]{:S(2)}) collective-permute-start(bf16[144,256]{1,0:T(8,128)(2,1)S(1)} %get-tuple-element.19), channel_id=1, source_target_pairs={{0,2},{2,0},{4,6},{6,4},{1,3},{3,1},{5,7},{7,5},{8,10},{10,8},{12,... | collective-permute-start | bytes 221192 | tf_op jit(solution)/shard_map/ppermute | solution.py:389
  22.6 8.4 %collective-permute-start.8 = (bf16[144,256]{1,0:T(8,128)(2,1)S(1)}, bf16[144,256]{1,0:T(8,128)(2,1)S(1)}, u32[]{:S(2)}, u32[]{:S(2)}) collective-permute-start(bf16[144,256]{1,0:T(8,128)(2,1)S(1)} %shard_map.73.rest_0_), channel_id=1, source_target_pairs={{0,4},{2,6},{4,0},{6,2},{1,5},{3,7},{5,1},{7,3},{8,12},{10,14},{12... | collective-permute-start | bytes 221192 | tf_op jit(solution)/shard_map/ppermute | solution.py:393
  25.5 8.6 %collective-permute-start.10 = (bf16[144,256]{1,0:T(8,128)(2,1)S(1)}, bf16[144,256]{1,0:T(8,128)(2,1)S(1)}, u32[]{:S(2)}, u32[]{:S(2)}) collective-permute-start(bf16[144,256]{1,0:T(8,128)(2,1)S(1)} %shard_map.74._), channel_id=1, source_target_pairs={{0,4},{2,6},{4,0},{6,2},{1,5},{3,7},{5,1},{7,3},{8,12},{10,14},{12... | collective-permute-start | bytes 221192 | tf_op jit(solution)/shard_map/ppermute | solution.py:401
  26.5 6.0 %collective-permute-start.7 = (bf16[512,256]{1,0:T(8,128)(2,1)S(1)}, bf16[512,256]{1,0:T(8,128)(2,1)S(1)}, u32[]{:S(2)}, u32[]{:S(2)}) collective-permute-start(bf16[512,256]{1,0:T(8,128)(2,1)S(1)} %get-tuple-element.22), channel_id=1, source_target_pairs={{0,1},{1,0},{2,3},{3,2},{4,5},{5,4},{6,7},{7,6},{8,9},{9,8},{10,11... | collective-permute-start | bytes 786440 | tf_op jit(solution)/shard_map/ppermute | solution.py:410
  26.6 8.0 %collective-permute-start.9 = (bf16[288,256]{1,0:T(8,128)(2,1)S(1)}, bf16[288,256]{1,0:T(8,128)(2,1)S(1)}, u32[]{:S(2)}, u32[]{:S(2)}) collective-permute-start(bf16[288,256]{1,0:T(8,128)(2,1)S(1)} %get-tuple-element.25), channel_id=1, source_target_pairs={{0,2},{2,0},{4,6},{6,4},{1,3},{3,1},{5,7},{7,5},{8,10},{10,8},{12,... | collective-permute-start | bytes 442376 | tf_op jit(solution)/shard_map/ppermute | solution.py:409

commit v2 on v1

--- a/solution.py
+++ b/solution.py
@@ -172,8 +172,8 @@
     image[:, pl.ds(1 + (1 - tile) * rows, rows)] = other[...]
 
 
-def first_kernel(out_ref):
-    out_ref[...] = jnp.zeros_like(out_ref)
+def order_kernel(*refs):
+    refs[-1][...] = jnp.zeros_like(refs[-1])
 
 
 def spatial_kernel(own, weight, other, _, pre_ref, act_ref, image, pre_all):
@@ -206,7 +206,8 @@
 def forward_sum_kernel(partial, arrived, *rest, first):
     sum_ref = rest[-1]
     rows = partial[first : first + sum_ref.shape[0]]
-    sum_ref[...] = (rows + arrived[...].astype(jnp.float32)).astype(sum_ref.dtype)
+    came = arrived[: sum_ref.shape[0]].astype(jnp.float32)
+    sum_ref[...] = (rows + came).astype(sum_ref.dtype)
 
 
 def last_sum_kernel(keep, near, last_a, last_b, _, out_ref, *, scale):
@@ -216,7 +217,7 @@
         out_ref[first : first + half] = (total + last[...].astype(jnp.float32)) * scale
 
 
-def transpose_kernel(own, other, out_ref, image):
+def transpose_kernel(own, other, _, out_ref, image):
     frames, rows, width, channels = own.shape
     tile = lax.axis_index("tile")
     whole_image(own, other, image)
@@ -231,10 +232,20 @@
     ext[2 * tile] = first[...]
     ext[1] = own[...]
     ext[2 - 2 * tile] = second[...]
+    chip = lax.axis_index("frame")
+
+    @pl.when(chip == 0)
+    def _():
+        ext[0] = jnp.zeros_like(ext[0])
+
+    @pl.when(chip == lax.axis_size("frame") - 1)
+    def _():
+        ext[2] = jnp.zeros_like(ext[2])
+
     return ext[...].reshape(-1, own.shape[1])
 
 
-def act_grad_kernel(own, first_in, second_in, weight, pre_ref, out_ref, ext):
+def act_grad_kernel(own, first_in, second_in, weight, pre_ref, _, out_ref, ext):
     count, channels = own.shape
     frames = slabs(own, first_in, second_in, ext)
     hop = count // 4
@@ -254,7 +265,7 @@
     out_ref[...] = (act_grad * (sig * (1.0 + pre * (1.0 - sig)))).astype(jnp.bfloat16)
 
 
-def temporal_kernel(feats, act, first_in, second_in, weight, out_ref, done_ref, ext):
+def temporal_kernel(feats, act, first_in, second_in, weight, _, out_ref, done_ref, ext):
     count, channels = feats.shape
     own = act.at[lax.axis_index("tile")]
     frames = slabs(own, first_in, second_in, ext)
@@ -299,7 +310,7 @@
         ref[...] = total[pl.ds(pl.multiple_of(first, 16), ref.shape[0])].astype(ref.dtype)
 
 
-def input_grad_kernel(out_grad, own, other, weight, _, out_ref, ext):
+def input_grad_kernel(out_grad, own, other, weight, _, out_ref, done_ref, ext):
     frames, rows, width, channels = own.shape
     with_edges(own, other, ext)
     after, same, before = column_shifts(ext[...].reshape(-1, channels), width)
@@ -315,6 +326,7 @@
                 preferred_element_type=jnp.float32,
             )
     out_ref[...] = total.astype(jnp.bfloat16)
+    done_ref[...] = jnp.zeros_like(done_ref)
 
 
 def per_device_pair(clip_feats, out_grad, spatial_weight, temporal_weight):
@@ -325,6 +337,7 @@
     scale = 1.0 / math.sqrt(frames * chips * rows * cores * width)
     outward = [(2 * z, 2 * z + 2) for z in range(chips - 1)]
     outward += [(2 * z + 3, 2 * z + 1) for z in range(chips - 1)]
+    outward += [(2 * chips - 2, 2 * chips - 1), (1, 0)]
     inward = [(target, source) for source, target in outward]
     both = ("frame", "tile")
     swap = [(0, 1), (1, 0)]
@@ -341,7 +354,7 @@
     grad_second = lax.ppermute(grad_flat, both, inward)
     feat_other = lax.ppermute(clip_feats, "tile", swap)
 
-    (first,) = kernel_call(first_kernel, [((8, 128), f32)], [], 2 * product)
+    (first,) = kernel_call(order_kernel, [((8, 128), f32)], [], 2 * product)
     pre, act = kernel_call(
         spatial_kernel,
         [(flat, f32), ((2, *flat), bf16)],
@@ -355,14 +368,14 @@
         [((2, 3 * channels, count), bf16)],
         [image],
         0,
-        clip_feats, feat_other,
+        clip_feats, feat_other, pre, anywhere=1,
     )
     (pre_grad,) = kernel_call(
         act_grad_kernel,
         [(flat, bf16)],
         [three],
         product,
-        grad_flat, grad_first, grad_second, temporal_weight, pre,
+        grad_flat, grad_first, grad_second, temporal_weight, pre, feats_t, anywhere=1,
     )
     pre_grad = pre_grad.reshape(clip_feats.shape)
     pre_other = lax.ppermute(pre_grad, "tile", swap)
@@ -388,7 +401,11 @@
     far_in_a = lax.ppermute(far_a, "frame", beside)
     far_in_b = lax.ppermute(far_b, "frame", beside)
     (sum_a,) = kernel_call(
-        functools.partial(forward_sum_kernel, first=0), [(half, bf16)], [], 0, onward, far_in_a
+        functools.partial(forward_sum_kernel, first=0),
+        [(half, bf16)],
+        [],
+        4 * product,
+        onward, far_in_a, act_in, anywhere=1,
     )
     last_a = lax.ppermute(sum_a, "frame", across)
     (sum_b,) = kernel_call(
@@ -409,19 +426,22 @@
     near_in = lax.ppermute(near, "frame", beside)
     act_second = lax.ppermute(act_pass, "tile", swap)
 
-    (input_grad,) = kernel_call(
+    input_grad, done = kernel_call(
         input_grad_kernel,
-        [(flat, bf16)],
+        [(flat, bf16), ((8, 128), f32)],
         [ext],
-        20 * product,
-        grad_flat, pre_grad, pre_other, spatial_weight, last_a, anywhere=1,
+        product,
+        grad_flat, pre_grad, pre_other, spatial_weight, sum_b, anywhere=1,
+    )
+    (arrived,) = kernel_call(
+        order_kernel, [((8, 128), f32)], [], 20 * product, last_a, done, anywhere=2
     )
     block_out, done = kernel_call(
         temporal_kernel,
         [(flat, bf16), ((8, 128), f32)],
         [three],
         product,
-        feat_flat, act, act_first, act_second, temporal_weight,
+        feat_flat, act, act_first, act_second, temporal_weight, arrived, anywhere=1,
     )
     (weight_grad,) = kernel_call(
         functools.partial(last_sum_kernel, scale=scale),

time: 35.6 us -> 34.4 us (0.966)
  starting transfers between devices: 19.2 us -> 12.4 us
  waiting for transfers between devices: 6.66 us -> 12.3 us
    ppermute x1, starting transfers between devices: 4.58 us -> 2.02 us  [per_device_pair(): act_in = lax.ppermute(act, both, outward)]
    ppermute x1, waiting for transfers between devices: 0.01 us -> 2.19 us  [per_device_pair(): grad_first = lax.ppermute(grad_flat, both, outward)]
    ppermute x1, waiting for transfers between devices: 0.78 us -> 2.94 us  [per_device_pair(): grad_second = lax.ppermute(grad_flat, both, inward)]
    ppermute x1, starting transfers between devices: 4.65 us -> 2.62 us  [per_device_pair(): grad_first = lax.ppermute(grad_flat, both, outward)]
    ppermute x1, starting transfers between devices: 1.29 us -> 0.01 us  [per_device_pair(): grad_second = lax.ppermute(grad_flat, both, inward)]
    ppermute x1, waiting for transfers between devices: 0.56 us -> 1.81 us  [per_device_pair(): near_in = lax.ppermute(near, 'frame', beside)]
    ppermute x1, starting transfers between devices: 2.08 us -> 1.28 us  [per_device_pair(): near_in = lax.ppermute(near, 'frame', beside)]
    ppermute x1, waiting for transfers between devices: 0.17 us -> 0.7 us  [per_device_pair(): pre_other = lax.ppermute(pre_grad, 'tile', swap)]
  transfers between devices with their start and end apart: 11 -> 11, of which waited for: 5 -> 6; matrix products, arithmetic and copies ran while one was open for 0% -> 0% of each run, Pallas kernels for 22% -> 23%
where the time goes in v2:
time: 34.4 us; the launch traced here: 34.2 us
  starting transfers between devices  12.4 us (36%)
  waiting for transfers between devices  12.3 us (36%)
  Pallas kernels  8.79 us (26%)
  between operations  0.74 us (2%)
    pallas_call x13, Pallas kernels, kernel_call(): pl.pallas_call(body, out_shape=tuple((jax.ShapeDtypeStruct(shape, kind) f...  8.79 us
    ppermute x1, starting transfers between devices, per_device_pair(): last_a = lax.ppermute(sum_a, 'frame', across)  2.96 us
    ppermute x1, waiting for transfers between devices, per_device_pair(): grad_second = lax.ppermute(grad_flat, both, inward)  2.94 us
    ppermute x1, waiting for transfers between devices, per_device_pair(): far_in_a = lax.ppermute(far_a, 'frame', beside)  2.75 us
    ppermute x1, starting transfers between devices, per_device_pair(): grad_first = lax.ppermute(grad_flat, both, outward)  2.62 us
    ppermute x1, waiting for transfers between devices, per_device_pair(): grad_first = lax.ppermute(grad_flat, both, outward)  2.19 us
    ppermute x1, starting transfers between devices, per_device_pair(): act_in = lax.ppermute(act, both, outward)  2.02 us
    ppermute x1, waiting for transfers between devices, per_device_pair(): last_a = lax.ppermute(sum_a, 'frame', across)  1.86 us
  transfers between devices with their start and end apart: 11, of which 6 were waited for; matrix products, arithmetic and copies ran while one was open for 0% of the time, Pallas kernels for 23%

profile of v2, /device:TPU:0, one launch (start us, length us, event | category | flops | bytes accessed | tf_op | source)
XLA Modules:
  0.0 34.2 jit_solution(11504190404879165545)
XLA Ops:
  0.6 0.5 %collective-permute-start = (bf16[8,4,16,256]{3,2,1,0:T(8,128)(2,1)}, bf16[8,4,16,256]{3,2,1,0:T(8,128)(2,1)S(1)}, u32[]{:S(2)}, u32[]{:S(2)}) collective-permute-start(bf16[8,4,16,256]{3,2,1,0:T(8,128)(2,1)} %own.3), channel_id=1, source_target_pairs={{0,1},{1,0},{2,3},{3,2},{4,5},{5,4},{6,7},{7,6},{8,9},{9,8},{10,11... | collective-permute-start | bytes 786440 | tf_op jit(solution)/shard_map/ppermute | solution.py:355
  1.1 0.0 copy-start.1
  1.1 0.0 copy-start.3
  1.2 2.6 %collective-permute-start.2 = (bf16[512,256]{1,0:T(8,128)(2,1)}, bf16[512,256]{1,0:T(8,128)(2,1)S(1)}, u32[]{:S(2)}, u32[]{:S(2)}) collective-permute-start(bf16[512,256]{1,0:T(8,128)(2,1)} %bitcast.9), channel_id=1, source_target_pairs={{0,2},{2,4},{4,6},{3,1},{5,3},{7,5},{6,7},{1,0},{8,10},{10,12},{12... | collective-permute-start | bytes 786440 | tf_op jit(solution)/shard_map/ppermute | solution.py:353
  3.8 0.0 collective-permute-start.3
  3.8 0.0 collective-permute-done.other
  3.8 0.0 copy-done.1
  3.8 0.0 copy-done.3
  3.8 1.7 %shard_map.68 = (f32[512,256]{1,0:T(8,128)S(1)}, bf16[2,512,256]{2,1,0:T(8,128)(2,1)S(1)}) custom-call(bf16[8,4,16,256]{3,2,1,0:T(8,128)(2,1)S(1)} %copy-done.1, bf16[2304,256]{1,0:T(8,128)(2,1)S(1)} %copy-done.3, bf16[8,4,16,256]{3,2,1,0:T(8,128)(2,1)S(1)} %collective-permute-done.other, f32[8,128]{1,0:T(8,128)S(1)} %shard_map.67._), custom_call_target="tpu_custom_call" | custom-call | flops 1207959552 | bytes 2756608 | tf_op jit(solution)/shard_map/pallas_call | solution.py:129
  5.5 0.0 copy-start
  5.5 0.0 copy-start.2
  5.6 2.0 %collective-permute-start.1 = (bf16[2,512,256]{2,1,0:T(8,128)(2,1)S(1)}, bf16[2,512,256]{2,1,0:T(8,128)(2,1)S(1)}, u32[]{:S(2)}, u32[]{:S(2)}) collective-permute-start(bf16[2,512,256]{2,1,0:T(8,128)(2,1)S(1)} %get-tuple-element.17.act), channel_id=1, source_target_pairs={{0,2},{2,4},{4,6},{3,1},{5,3},{7,5},{6,7},{1,0},{8,10},{10,12},{12... | collective-permute-start | bytes 1572872 | tf_op jit(solution)/shard_map/ppermute | solution.py:365
  7.6 0.5 %shard_map.69._.feats_t = bf16[2,768,512]{2,1,0:T(8,128)(2,1)S(1)} custom-call(bf16[8,4,16,256]{3,2,1,0:T(8,128)(2,1)S(1)} %copy-done.1, bf16[8,4,16,256]{3,2,1,0:T(8,128)(2,1)S(1)} %collective-permute-done.other, f32[512,256]{1,0:T(8,128)S(1)} %get-tuple-element.18._.pre_ref), custom_call_target="tpu_custom_call" | custom-call | bytes 2621440 | tf_op jit(solution)/shard_map/pallas_call | solution.py:129
  8.1 2.2 %collective-permute-done.2.first_in = bf16[512,256]{1,0:T(8,128)(2,1)S(1)} collective-permute-done((bf16[512,256]{1,0:T(8,128)(2,1)}, bf16[512,256]{1,0:T(8,128)(2,1)S(1)}, u32[]{:S(2)}, u32[]{:S(2)}) %collective-permute-start.2) | collective-permute-done | bytes 262176 | tf_op jit(solution)/shard_map/ppermute | solution.py:353
  10.3 2.9 %collective-permute-done.3.second_in = bf16[512,256]{1,0:T(8,128)(2,1)S(1)} collective-permute-done((bf16[512,256]{1,0:T(8,128)(2,1)}, bf16[512,256]{1,0:T(8,128)(2,1)S(1)}, u32[]{:S(2)}, u32[]{:S(2)}) %collective-permute-start.3) | collective-permute-done | bytes 262176 | tf_op jit(solution)/shard_map/ppermute | solution.py:354
  13.2 0.0 copy-done
  13.2 0.0 copy-done.2
  13.2 0.9 %shard_map.70 = bf16[512,256]{1,0:T(8,128)(2,1)S(1)} custom-call(bf16[512,256]{1,0:T(8,128)(2,1)S(1)} %bitcast.11, bf16[512,256]{1,0:T(8,128)(2,1)S(1)} %collective-permute-done.2.first_in, bf16[512,256]{1,0:T(8,128)(2,1)S(1)} %collective-permute-done.3.second_in, bf16[2304,256]{1,0:T(8,128)(2,1)S(1)} %copy-done, ...), custom_call_target="tpu_custom_call" | custom-call | flops 603979776 | bytes 4325376 | tf_op jit(solution)/shard_map/pallas_call | solution.py:129
  14.1 0.1 collective-permute-start.4
  14.2 0.8 %shard_map.71.term = f32[3,768,256]{2,1,0:T(8,128)S(1)} custom-call(bf16[2,768,512]{2,1,0:T(8,128)(2,1)S(1)} %shard_map.69._.feats_t, bf16[8,4,16,256]{3,2,1,0:T(8,128)(2,1)S(1)} %bitcast.7), custom_call_target="tpu_custom_call" | custom-call | flops 603979776 | bytes 4194304 | tf_op jit(solution)/shard_map/pallas_call | solution.py:129
  15.0 0.7 %collective-permute-done.4.other = bf16[8,4,16,256]{3,2,1,0:T(8,128)(2,1)S(1)} collective-permute-done((bf16[8,4,16,256]{3,2,1,0:T(8,128)(2,1)S(1)}, bf16[8,4,16,256]{3,2,1,0:T(8,128)(2,1)S(1)}, u32[]{:S(2)}, u32[]{:S(2)}) %collective-permute-start.4) | collective-permute-done | bytes 262176 | tf_op jit(solution)/shard_map/ppermute | solution.py:381
  15.7 0.9 %shard_map.72 = (bf16[144,256]{1,0:T(8,128)(2,1)S(1)}, bf16[144,256]{1,0:T(8,128)(2,1)S(1)}, f32[288,256]{1,0:T(8,128)S(1)}, bf16[288,256]{1,0:T(8,128)(2,1)S(1)}, f32[288,256]{1,0:T(8,128)S(1)}) custom-call(bf16[2,768,512]{2,1,0:T(8,128)(2,1)S(1)} %shard_map.69._.feats_t, bf16[8,4,16,256]{3,2,1,0:T(8,128)(2,1)S(1)} %collective-permute-done.4.other, ...), custom_call_target="tpu_custom_call" | custom-call | flops 603979776 | bytes 5079040 | tf_op jit(solution)/shard_map/pallas_call | solution.py:129
  16.6 1.6 %collective-permute-start.6 = (bf16[144,256]{1,0:T(8,128)(2,1)S(1)}, bf16[144,256]{1,0:T(8,128)(2,1)S(1)}, u32[]{:S(2)}, u32[]{:S(2)}) collective-permute-start(bf16[144,256]{1,0:T(8,128)(2,1)S(1)} %get-tuple-element.22), channel_id=1, source_target_pairs={{0,2},{2,0},{4,6},{6,4},{1,3},{3,1},{5,7},{7,5},{8,10},{10,8},{12,... | collective-permute-start | bytes 221192 | tf_op jit(solution)/shard_map/ppermute | solution.py:401
  18.2 0.5 %collective-permute-start.5 = (bf16[144,256]{1,0:T(8,128)(2,1)S(1)}, bf16[144,256]{1,0:T(8,128)(2,1)S(1)}, u32[]{:S(2)}, u32[]{:S(2)}) collective-permute-start(bf16[144,256]{1,0:T(8,128)(2,1)S(1)} %get-tuple-element.21), channel_id=1, source_target_pairs={{0,2},{2,0},{4,6},{6,4},{1,3},{3,1},{5,7},{7,5},{8,10},{10,8},{12,... | collective-permute-start | bytes 221192 | tf_op jit(solution)/shard_map/ppermute | solution.py:402
  18.7 2.7 %collective-permute-done.6.arrived = bf16[144,256]{1,0:T(8,128)(2,1)S(1)} collective-permute-done((bf16[144,256]{1,0:T(8,128)(2,1)S(1)}, bf16[144,256]{1,0:T(8,128)(2,1)S(1)}, u32[]{:S(2)}, u32[]{:S(2)}) %collective-permute-start.6) | collective-permute-done | bytes 73760 | tf_op jit(solution)/shard_map/ppermute | solution.py:401
  21.5 0.0 collective-permute-done.1.rest_0_.arrived
  21.5 3.0 %collective-permute-start.8 = (bf16[144,256]{1,0:T(8,128)(2,1)S(1)}, bf16[144,256]{1,0:T(8,128)(2,1)S(1)}, u32[]{:S(2)}, u32[]{:S(2)}) collective-permute-start(bf16[144,256]{1,0:T(8,128)(2,1)S(1)} %shard_map.73.rest_0_), channel_id=1, source_target_pairs={{0,4},{2,6},{4,0},{6,2},{1,5},{3,7},{5,1},{7,3},{8,12},{10,14},{12... | collective-permute-start | bytes 221192 | tf_op jit(solution)/shard_map/ppermute | solution.py:410
  24.5 0.0 collective-permute-done.5.arrived
  24.5 0.8 %collective-permute-start.10 = (bf16[144,256]{1,0:T(8,128)(2,1)S(1)}, bf16[144,256]{1,0:T(8,128)(2,1)S(1)}, u32[]{:S(2)}, u32[]{:S(2)}) collective-permute-start(bf16[144,256]{1,0:T(8,128)(2,1)S(1)} %shard_map.74._), channel_id=1, source_target_pairs={{0,4},{2,6},{4,0},{6,2},{1,5},{3,7},{5,1},{7,3},{8,12},{10,14},{12... | collective-permute-start | bytes 221192 | tf_op jit(solution)/shard_map/ppermute | solution.py:418
  25.3 0.1 collective-permute-start.7
  25.4 1.3 %collective-permute-start.9 = (bf16[288,256]{1,0:T(8,128)(2,1)S(1)}, bf16[288,256]{1,0:T(8,128)(2,1)S(1)}, u32[]{:S(2)}, u32[]{:S(2)}) collective-permute-start(bf16[288,256]{1,0:T(8,128)(2,1)S(1)} %get-tuple-element.29), channel_id=1, source_target_pairs={{0,2},{2,0},{4,6},{6,4},{1,3},{3,1},{5,7},{7,5},{8,10},{10,8},{12,... | collective-permute-start | bytes 442376 | tf_op jit(solution)/shard_map/ppermute | solution.py:426
  26.6 1.5 %shard_map.76 = (bf16[512,256]{1,0:T(8,128)(2,1)}, f32[8,128]{1,0:T(8,128)S(1)}) custom-call(bf16[512,256]{1,0:T(8,128)(2,1)S(1)} %bitcast.12, bf16[8,4,16,256]{3,2,1,0:T(8,128)(2,1)S(1)} %bitcast.8, bf16[8,4,16,256]{3,2,1,0:T(8,128)(2,1)S(1)} %collective-permute-done.4.other, bf16[2304,256]{1,0:T(8,128)(2,1)S(1)} %copy-done.3, bf16[144,256]{1,0:T(8,128)(2,1)S(1)} %shard_map.74._), custom_call_target="tpu_custom_call" | custom-call | flops 603979776 | bytes 2306048 | tf_op jit(solution)/shard_map/pallas_call | solution.py:129
  28.2 1.9 %collective-permute-done.8.refs_0_.last_a = bf16[144,256]{1,0:T(8,128)(2,1)S(1)} collective-permute-done((bf16[144,256]{1,0:T(8,128)(2,1)S(1)}, bf16[144,256]{1,0:T(8,128)(2,1)S(1)}, u32[]{:S(2)}, u32[]{:S(2)}) %collective-permute-start.8) | collective-permute-done | bytes 73760 | tf_op jit(solution)/shard_map/ppermute | solution.py:410
  30.1 0.0 collective-permute-done.7.second_in
  30.1 1.6 %shard_map.78 = (bf16[512,256]{1,0:T(8,128)(2,1)}, f32[8,128]{1,0:T(8,128)S(1)}) custom-call(bf16[512,256]{1,0:T(8,128)(2,1)S(1)} %bitcast.5, bf16[2,512,256]{2,1,0:T(8,128)(2,1)S(1)} %get-tuple-element.17.act, bf16[512,256]{1,0:T(8,128)(2,1)S(1)} %get-tuple-element.23.first_in, bf16[512,256]{1,0:T(8,128)(2,1)S(1)} %collective-permute-done.7.second_in, ...), custom_call_target="tpu_custom_call" | custom-call | flops 603979776 | bytes 2760704 | tf_op jit(solution)/shard_map/pallas_call | solution.py:129
  31.6 0.0 collective-permute-done.10.last_b
  31.6 1.8 %collective-permute-done.9.near = bf16[288,256]{1,0:T(8,128)(2,1)S(1)} collective-permute-done((bf16[288,256]{1,0:T(8,128)(2,1)S(1)}, bf16[288,256]{1,0:T(8,128)(2,1)S(1)}, u32[]{:S(2)}, u32[]{:S(2)}) %collective-permute-start.9) | collective-permute-done | bytes 147488 | tf_op jit(solution)/shard_map/ppermute | solution.py:426
  33.4 0.8 %shard_map.79 = f32[288,256]{1,0:T(8,128)} custom-call(f32[288,256]{1,0:T(8,128)S(1)} %get-tuple-element.28.keep, bf16[288,256]{1,0:T(8,128)(2,1)S(1)} %collective-permute-done.9.near, bf16[144,256]{1,0:T(8,128)(2,1)S(1)} %collective-permute-done.8.refs_0_.last_a, bf16[144,256]{1,0:T(8,128)(2,1)S(1)} %collective-permute-done.10.last_b, ...), custom_call_target="tpu_custom_call" | custom-call | bytes 888832 | tf_op jit(solution)/shard_map/pallas_call | solution.py:129
  (5 shorter events, 0.1 us)
Async XLA Ops:
  0.6 3.1 %collective-permute-start = (bf16[8,4,16,256]{3,2,1,0:T(8,128)(2,1)}, bf16[8,4,16,256]{3,2,1,0:T(8,128)(2,1)S(1)}, u32[]{:S(2)}, u32[]{:S(2)}) collective-permute-start(bf16[8,4,16,256]{3,2,1,0:T(8,128)(2,1)} %own.3), channel_id=1, source_target_pairs={{0,1},{1,0},{2,3},{3,2},{4,5},{5,4},{6,7},{7,6},{8,9},{9,8},{10,11... | collective-permute-start | bytes 786440 | tf_op jit(solution)/shard_map/ppermute | solution.py:355
  1.1 2.6 %copy-start.1 = (bf16[8,4,16,256]{3,2,1,0:T(8,128)(2,1)S(1)}, bf16[8,4,16,256]{3,2,1,0:T(8,128)(2,1)}, u32[]{:S(2)}) copy-start(bf16[8,4,16,256]{3,2,1,0:T(8,128)(2,1)} %own.3) | copy-start | bytes 786436
  1.1 2.6 %copy-start.3 = (bf16[2304,256]{1,0:T(8,128)(2,1)S(1)}, bf16[2304,256]{1,0:T(8,128)(2,1)}, u32[]{:S(2)}) copy-start(bf16[2304,256]{1,0:T(8,128)(2,1)} %weight.6) | copy-start | bytes 3538948
  1.2 9.1 %collective-permute-start.2 = (bf16[512,256]{1,0:T(8,128)(2,1)}, bf16[512,256]{1,0:T(8,128)(2,1)S(1)}, u32[]{:S(2)}, u32[]{:S(2)}) collective-permute-start(bf16[512,256]{1,0:T(8,128)(2,1)} %bitcast.9), channel_id=1, source_target_pairs={{0,2},{2,4},{4,6},{3,1},{5,3},{7,5},{6,7},{1,0},{8,10},{10,12},{12... | collective-permute-start | bytes 786440 | tf_op jit(solution)/shard_map/ppermute | solution.py:353
  3.8 9.5 %collective-permute-start.3 = (bf16[512,256]{1,0:T(8,128)(2,1)}, bf16[512,256]{1,0:T(8,128)(2,1)S(1)}, u32[]{:S(2)}, u32[]{:S(2)}) collective-permute-start(bf16[512,256]{1,0:T(8,128)(2,1)} %bitcast.10), channel_id=1, source_target_pairs={{2,0},{4,2},{6,4},{1,3},{3,5},{5,7},{7,6},{0,1},{10,8},{12,10},{14... | collective-permute-start | bytes 786440 | tf_op jit(solution)/shard_map/ppermute | solution.py:354
  5.5 7.7 %copy-start = (bf16[2304,256]{1,0:T(8,128)(2,1)S(1)}, bf16[2304,256]{1,0:T(8,128)(2,1)}, u32[]{:S(2)}) copy-start(bf16[2304,256]{1,0:T(8,128)(2,1)} %weight.7) | copy-start | bytes 3538948
  5.5 7.7 %copy-start.2 = (bf16[8,4,16,256]{3,2,1,0:T(8,128)(2,1)S(1)}, bf16[8,4,16,256]{3,2,1,0:T(8,128)(2,1)}, u32[]{:S(2)}) copy-start(bf16[8,4,16,256]{3,2,1,0:T(8,128)(2,1)} %param.5) | copy-start | bytes 786436
  5.6 15.9 %collective-permute-start.1 = (bf16[2,512,256]{2,1,0:T(8,128)(2,1)S(1)}, bf16[2,512,256]{2,1,0:T(8,128)(2,1)S(1)}, u32[]{:S(2)}, u32[]{:S(2)}) collective-permute-start(bf16[2,512,256]{2,1,0:T(8,128)(2,1)S(1)} %get-tuple-element.17.act), channel_id=1, source_target_pairs={{0,2},{2,4},{4,6},{3,1},{5,3},{7,5},{6,7},{1,0},{8,10},{10,12},{12... | collective-permute-start | bytes 1572872 | tf_op jit(solution)/shard_map/ppermute | solution.py:365
  14.1 1.6 %collective-permute-start.4 = (bf16[8,4,16,256]{3,2,1,0:T(8,128)(2,1)S(1)}, bf16[8,4,16,256]{3,2,1,0:T(8,128)(2,1)S(1)}, u32[]{:S(2)}, u32[]{:S(2)}) collective-permute-start(bf16[8,4,16,256]{3,2,1,0:T(8,128)(2,1)S(1)} %bitcast.6), channel_id=1, source_target_pairs={{0,1},{1,0},{2,3},{3,2},{4,5},{5,4},{6,7},{7,6},{8,9},{9,8},{10,11... | collective-permute-start | bytes 786440 | tf_op jit(solution)/shard_map/ppermute | solution.py:381
  16.6 4.8 %collective-permute-start.6 = (bf16[144,256]{1,0:T(8,128)(2,1)S(1)}, bf16[144,256]{1,0:T(8,128)(2,1)S(1)}, u32[]{:S(2)}, u32[]{:S(2)}) collective-permute-start(bf16[144,256]{1,0:T(8,128)(2,1)S(1)} %get-tuple-element.22), channel_id=1, source_target_pairs={{0,2},{2,0},{4,6},{6,4},{1,3},{3,1},{5,7},{7,5},{8,10},{10,8},{12,... | collective-permute-start | bytes 221192 | tf_op jit(solution)/shard_map/ppermute | solution.py:401
  18.2 6.2 %collective-permute-start.5 = (bf16[144,256]{1,0:T(8,128)(2,1)S(1)}, bf16[144,256]{1,0:T(8,128)(2,1)S(1)}, u32[]{:S(2)}, u32[]{:S(2)}) collective-permute-start(bf16[144,256]{1,0:T(8,128)(2,1)S(1)} %get-tuple-element.21), channel_id=1, source_target_pairs={{0,2},{2,0},{4,6},{6,4},{1,3},{3,1},{5,7},{7,5},{8,10},{10,8},{12,... | collective-permute-start | bytes 221192 | tf_op jit(solution)/shard_map/ppermute | solution.py:402
  21.5 8.6 %collective-permute-start.8 = (bf16[144,256]{1,0:T(8,128)(2,1)S(1)}, bf16[144,256]{1,0:T(8,128)(2,1)S(1)}, u32[]{:S(2)}, u32[]{:S(2)}) collective-permute-start(bf16[144,256]{1,0:T(8,128)(2,1)S(1)} %shard_map.73.rest_0_), channel_id=1, source_target_pairs={{0,4},{2,6},{4,0},{6,2},{1,5},{3,7},{5,1},{7,3},{8,12},{10,14},{12... | collective-permute-start | bytes 221192 | tf_op jit(solution)/shard_map/ppermute | solution.py:410
  24.5 7.1 %collective-permute-start.10 = (bf16[144,256]{1,0:T(8,128)(2,1)S(1)}, bf16[144,256]{1,0:T(8,128)(2,1)S(1)}, u32[]{:S(2)}, u32[]{:S(2)}) collective-permute-start(bf16[144,256]{1,0:T(8,128)(2,1)S(1)} %shard_map.74._), channel_id=1, source_target_pairs={{0,4},{2,6},{4,0},{6,2},{1,5},{3,7},{5,1},{7,3},{8,12},{10,14},{12... | collective-permute-start | bytes 221192 | tf_op jit(solution)/shard_map/ppermute | solution.py:418
  25.3 4.8 %collective-permute-start.7 = (bf16[512,256]{1,0:T(8,128)(2,1)S(1)}, bf16[512,256]{1,0:T(8,128)(2,1)S(1)}, u32[]{:S(2)}, u32[]{:S(2)}) collective-permute-start(bf16[512,256]{1,0:T(8,128)(2,1)S(1)} %get-tuple-element.24), channel_id=1, source_target_pairs={{0,1},{1,0},{2,3},{3,2},{4,5},{5,4},{6,7},{7,6},{8,9},{9,8},{10,11... | collective-permute-start | bytes 786440 | tf_op jit(solution)/shard_map/ppermute | solution.py:427
  25.4 8.1 %collective-permute-start.9 = (bf16[288,256]{1,0:T(8,128)(2,1)S(1)}, bf16[288,256]{1,0:T(8,128)(2,1)S(1)}, u32[]{:S(2)}, u32[]{:S(2)}) collective-permute-start(bf16[288,256]{1,0:T(8,128)(2,1)S(1)} %get-tuple-element.29), channel_id=1, source_target_pairs={{0,2},{2,0},{4,6},{6,4},{1,3},{3,1},{5,7},{7,5},{8,10},{10,8},{12,... | collective-permute-start | bytes 442376 | tf_op jit(solution)/shard_map/ppermute | solution.py:426
